TPU v7x, 32 devices: a whole 2x2x4 slice. The times are simulated.
32 devices in a mesh: cell: 8 (over y, x, core), lane: 4 (over z).
Axes of the slice: x: 2, y: 2, z: 4, core: 2. Of those that a mesh axis runs over, the one named last changes fastest.
Arguments:
- channel: float32 [8, 64, 2, 16, 256], P('cell', 'lane'), may hold values from -8 to 8
- symbols: bfloat16 [8, 16, 2, 2, 3072], P('cell'), may hold values from -4 to 4
- layers: int32 [8, 256], P('cell'), may hold values from 0 to 16, as said below
- user_ids: int32 [8, 16, 256], P('cell'), may hold values from 0 to 127
- user_power: float32 [8, 128], P('cell'), may hold values from 0.25 to 4
- neighbours: int32 [8, 6], replicated, may hold values from 0 to 7, as said below
- coupling: float32 [8, 6], replicated, may hold values from 0.05 to 0.5
Outputs:
- time_samples: float32 [8, 64, 2, 2, 4096], P('cell', 'lane')
Inputs may be any that keep to these rules, and one draw needn't show every extreme that they name: Some block of some cell has all 16 layers granted; for every index of the cell axis and every group of 32 aligned blocks, the layers of that index's 1 cells over the group sum to at most 192, and to exactly 192 for some index and group. `neighbours`: a cell never lists itself.
All inputs are finite; a program needn't handle non-finite values.
Results may differ from a plain program's by a relative error of at most 0.0029.
Values may be sent and summed in bfloat16 or wider, within the bound.
No kernel may reach another device: no remote copies, remote signals or barrier semaphores. Data moves between devices by JAX's collectives and lax.ppermute only.
A program may use at most 64 MiB of HBM per device.

v0:
```python
import functools
import math

import jax
import jax.numpy as jnp
import numpy as np
from jax import lax
from jax.experimental import pallas as pl
from jax.experimental.pallas import tpu as pltpu
from jax.sharding import PartitionSpec as P

NFFT = 4096
NS_STEPS = 6
NORM_EPS = 1e-06
NOISE_FLOOR = 0.05
WIDE = 128
HALF = WIDE // 2
ROWS = 8

VMEM = pl.BlockSpec(memory_space=pltpu.VMEM)
SMEM = pl.BlockSpec(memory_space=pltpu.SMEM)


def lane_iota():
    return lax.broadcasted_iota(jnp.int32, (ROWS, WIDE), 1)


def row_iota():
    return lax.broadcasted_iota(jnp.int32, (ROWS, WIDE), 0)


def turn(value, shift):
    shift = shift % WIDE
    return value if shift == 0 else pltpu.roll(value, shift, 1)


def params(mib):
    return pltpu.CompilerParams(vmem_limit_bytes=mib * 1024 * 1024)


def power_kernel(layers_ref, ids_ref, power_ref, amp_ref, own_ref, *, chunk):
    order, blocks = ids_ref.shape
    users = power_ref.shape[1]
    rooted = jnp.sqrt(power_ref[...])
    sums = []
    for t in range(blocks // WIDE):
        spot = pl.ds(t * WIDE, WIDE)
        granted = layers_ref[:, spot]
        total = jnp.zeros((ROWS, WIDE), jnp.float32)
        for h in range(order // ROWS):
            ids = ids_ref[pl.ds(h * ROWS, ROWS), spot]
            picked = jnp.zeros((ROWS, WIDE), jnp.float32)
            for u in range(users // WIDE):
                table = jnp.broadcast_to(rooted[:, u * WIDE : (u + 1) * WIDE], (ROWS, WIDE))
                found = jnp.take_along_axis(table, ids % WIDE, axis=1, mode="promise_in_bounds")
                picked = jnp.where(ids // WIDE == u, found, picked)
            amp = jnp.where(row_iota() + h * ROWS < granted, picked, 0.0)
            amp_ref[pl.ds(h * ROWS, ROWS), spot] = amp
            total = total + amp * amp
        sums.append(jnp.sum(total, axis=0, keepdims=True) / order)
    start = lax.axis_index("lane") * chunk
    mine = jnp.broadcast_to(sums[0], (ROWS, WIDE))
    for t in range(1, len(sums)):
        mine = jnp.where(start // WIDE == t, jnp.broadcast_to(sums[t], (ROWS, WIDE)), mine)
    shift = lax.rem(start, WIDE)
    mine = pltpu.roll(mine, lax.rem(WIDE - shift, WIDE), 1)
    both = jnp.where(lane_iota() < HALF, mine, pltpu.roll(mine, HALF, 1))
    own_ref[...] = both[0:1]


def gram_kernel(channel_ref, layers_ref, out_ref, *, chunk):
    antennas, _, order, blocks = channel_ref.shape
    low = lane_iota() < HALF
    rows = row_iota()
    for t in range(blocks // WIDE):
        spot = pl.ds(t * WIDE, WIDE)
        granted = layers_ref[:, spot]
        inside = [rows + h * ROWS < granted for h in range(2)]
        for base in range(0, ROWS, 2):
            tops = (base, base + 1)
            acc = {}

            def add(key, value):
                acc[key] = value if key not in acc else acc[key] + value

            for a in range(antennas):
                re = [channel_ref[a, 0, pl.ds(h * ROWS, ROWS), spot] for h in range(2)]
                im = [channel_ref[a, 1, pl.ds(h * ROWS, ROWS), spot] for h in range(2)]
                for l in tops:
                    lre = channel_ref[a, 0, pl.ds(l, 1), spot]
                    lim = channel_ref[a, 1, pl.ds(l, 1), spot]
                    add((l, "re", 0), lre * re[0] + lim * im[0])
                    add((l, "re", 1), lre * re[1] + lim * im[1])
                    add((l, "im", 0), lim * re[0] - lre * im[0])
                    g = l + ROWS
                    gre = channel_ref[a, 0, pl.ds(g, 1), spot]
                    gim = channel_ref[a, 1, pl.ds(g, 1), spot]
                    add((g, "re", 1), gre * re[1] + gim * im[1])
                    add((g, "im", 0), gim * re[0] - gre * im[0])
                    add((g, "im", 1), gim * re[1] - gre * im[1])
            for l in tops:
                g = l + ROWS
                here = granted > l
                there = granted > g
                upper = [
                    jnp.where(rows >= l, acc[l, "re", 0], acc[l, "im", 0]),
                    acc[l, "re", 1],
                ]
                lower = [
                    acc[g, "im", 0],
                    jnp.where(rows >= l, acc[g, "re", 1], acc[g, "im", 1]),
                ]
                for h in range(2):
                    top = jnp.where(jnp.logical_and(inside[h], here), upper[h], 0.0)
                    bottom = jnp.where(jnp.logical_and(inside[h], there), lower[h], 0.0)
                    for z in range(t * WIDE // chunk, (t + 1) * WIDE // chunk):
                        off = z * chunk - t * WIDE
                        out_ref[z, pl.ds(l * 2 * ROWS + h * ROWS, ROWS), :] = jnp.where(
                            low, turn(top, -off), turn(bottom, HALF - off)
                        )


def solve_kernel(
    neigh_ref, coup_ref, parts_ref, trans_ref, out_ref, pack, gram, e_a, e_b, s_a, s_b, d_re, d_im
):
    order = 2 * ROWS
    low = lane_iota() < HALF
    rows = row_iota()
    sign = jnp.where(low, -1.0, 1.0)

    def at(l, h):
        return pl.ds(l * order + h * ROWS, ROWS)

    def column(l, h):
        return pl.ds(h * ROWS * order + l, ROWS, stride=order)

    def row(ref, l, k):
        return ref[pl.ds(l * order + k, 1), :]

    for l in range(ROWS):
        for h in range(2):
            value = parts_ref[0, at(l, h), :]
            for z in range(1, parts_ref.shape[0]):
                value = value + parts_ref[z, at(l, h), :]
            other = pltpu.roll(value, HALF, 1)
            pack[at(l, h), :] = jnp.where(low, value, other)
            pack[at(l + ROWS, h), :] = jnp.where(low, other, value)

    cell = lax.axis_index("cell")
    sigma = jnp.full((1, WIDE), NOISE_FLOOR, jnp.float32)
    for k in range(neigh_ref.shape[1]):
        sigma = sigma + coup_ref[cell, k] * trans_ref[pl.ds(neigh_ref[cell, k], 1), :]

    trace = order * sigma
    for l in range(order):
        trace = trace + row(pack, l, l)
    inverse = 1.0 / trace
    kept = 1.0 - sigma * inverse

    for l in range(order):
        for h in range(2):
            here = pack[at(l, h), :]
            across = pack[column(l, h), :]
            above = jnp.where(low, here, -across)
            below = jnp.where(low, across, here)
            if h * ROWS > l:
                value = above
            elif h * ROWS + ROWS - 1 < l:
                value = below
            else:
                value = jnp.where(rows + h * ROWS >= l, above, below)
                value = jnp.where(jnp.logical_and(rows + h * ROWS == l, ~low), 0.0, value)
            gram[at(l, h), :] = value
            error = -value * inverse
            total = error
            if h * ROWS <= l < h * ROWS + ROWS:
                spot = jnp.logical_and(rows + h * ROWS == l, low)
                error = error + jnp.where(spot, kept, 0.0)
                total = error + jnp.where(spot, 1.0, 0.0)
            e_a[at(l, h), :] = error
            s_a[at(l, h), :] = total

    def spread(ref):
        for l in range(order):
            for h in range(2):
                value = ref[at(l, h), :]
                other = pltpu.roll(value, HALF, 1)
                d_re[at(l, h), :] = jnp.where(low, value, other)
                d_im[at(l, h), :] = jnp.where(low, other, value)

    def products(jobs):
        for base in range(0, order, 2):
            halves = (0, 1) if base < ROWS else (1,)
            plain, crossed = {}, {}
            for l in (base, base + 1):
                for j, (_, _, start) in enumerate(jobs):
                    for h in halves:
                        if start is not None:
                            plain[l, j, h] = start[at(l, h), :]
            for k in range(order):
                right = {
                    (j, h): ref[at(k, h), :] for j, (ref, _, _) in enumerate(jobs) for h in halves
                }
                for l in (base, base + 1):
                    left_re = row(d_re, l, k)
                    left_im = row(d_im, l, k) if k != l else None
                    for (j, h), value in right.items():
                        key = (l, j, h)
                        term = left_re * value
                        plain[key] = plain[key] + term if key in plain else term
                        if left_im is not None:
                            term = left_im * value
                            crossed[key] = crossed[key] + term if key in crossed else term
            for (l, j, h), value in plain.items():
                cross = pltpu.roll(crossed[l, j, h], HALF, 1)
                jobs[j][1][at(l, h), :] = value + sign * cross
        for _, ref, _ in jobs:
            for l in range(ROWS, order):
                ref[at(l, 0), :] = -sign * ref[column(l, 0), :]

    spread(e_a)
    products([(e_a, e_b, None)])

    def two_steps(_, carry):
        spread(e_b)
        products([(e_b, e_a, None), (s_a, s_b, s_a)])
        spread(e_a)
        products([(e_a, e_b, None), (s_b, s_a, s_b)])
        return carry

    lax.fori_loop(0, (NS_STEPS - 2) // 2, two_steps, 0)
    spread(e_b)
    products([(s_a, s_b, s_a)])

    for l in range(order):
        for h in range(2):
            s_a[at(l, h), :] = s_b[at(l, h), :] * inverse
    spread(s_a)
    products([(gram, e_a, None)])

    energy = []
    for h in range(2):
        value = s_a[at(0, h), :] * e_a[at(0, h), :]
        for m in range(1, order):
            value = value + s_a[at(m, h), :] * e_a[at(m, h), :]
        energy.append(value + pltpu.roll(value, HALF, 1))
    last = jnp.where(low, energy[0], energy[1])
    for l in range(ROWS):
        for h in range(2):
            first = s_a[at(l, h), :]
            second = s_a[at(l + ROWS, h), :]
            where = rows + h * ROWS
            value = jnp.where(
                low,
                jnp.where(where >= l, first, pltpu.roll(first, HALF, 1)),
                jnp.where(where >= l + ROWS, pltpu.roll(second, HALF, 1), second),
            )
            for z in range(out_ref.shape[0]):
                out_ref[z, at(l, h), :] = value
    for z in range(out_ref.shape[0]):
        out_ref[z, pl.ds(order * ROWS, ROWS), :] = last


def arrange_kernel(symbols_ref, order_ref, channel_ref, sym_ref, chan_ref, stage):
    antennas, _, layers, blocks = channel_ref.shape
    tiles = blocks // WIDE
    span = symbols_ref.shape[1] // tiles
    for t in range(tiles):
        piece = symbols_ref[:, pl.ds(t * span, span)]
        for k in range(span // WIDE // 2):
            got = jnp.dot(
                piece,
                order_ref[:, pl.ds(k * 2 * WIDE, 2 * WIDE)],
                preferred_element_type=jnp.float32,
            )
            sym_ref[t, 2 * k] = got[:, :WIDE]
            sym_ref[t, 2 * k + 1] = got[:, WIDE:]
    for t in range(tiles):
        for a in range(antennas):
            for r in range(2):
                for h in range(layers // ROWS):
                    stage[t, pl.ds((a * 2 + r) * layers + h * ROWS, ROWS), :] = channel_ref[
                        a, r, pl.ds(h * ROWS, ROWS), pl.ds(t * WIDE, WIDE)
                    ]
        for r in range(2):
            for m in range(layers):
                for h in range(antennas // ROWS):
                    first = h * ROWS * 2 * layers + r * layers + m
                    chan_ref[t, r, m, pl.ds(h * ROWS, ROWS), :] = stage[
                        t, pl.ds(first, ROWS, stride=2 * layers), :
                    ]


def transmit_kernel(
    packs_ref,
    amp_ref,
    chan_ref,
    sym_ref,
    high_ref,
    rest_ref,
    twist_ref,
    out_ref,
    pack,
    scale,
    weight,
    grid_high,
    grid_rest,
    spec,
    *,
    chunk,
):
    tiles, _, order, antennas, _ = chan_ref.shape
    per_block, syms = sym_ref.shape[1], sym_ref.shape[2] // (2 * order)
    groups = antennas // ROWS
    lanes = lane_iota()

    for t in range(tiles):
        for i in range(2 * ROWS + 1):
            rows = pl.ds(i * ROWS, ROWS)
            first = second = None
            for z in range(t * WIDE // chunk, (t + 1) * WIDE // chunk):
                off = z * chunk - t * WIDE
                value = packs_ref[z, rows, :]
                if first is None:
                    first, second = value, pltpu.roll(value, HALF, 1)
                else:
                    first = jnp.where(lanes >= off, turn(value, off), first)
                    second = jnp.where(lanes >= off, turn(value, off - HALF), second)
            if i < 2 * ROWS:
                pack[t, rows, :] = first
                pack[t, pl.ds((i + 2 * ROWS) * ROWS, ROWS), :] = second
            else:
                for h, energy in enumerate((first, second)):
                    amp = amp_ref[pl.ds(h * ROWS, ROWS), pl.ds(t * WIDE, WIDE)]
                    scale[t, pl.ds(h * ROWS, ROWS), :] = amp / jnp.sqrt(energy + NORM_EPS)

    def row(t, l, m):
        return pack[t, pl.ds(l * order + m, 1), :]

    for t in range(tiles):
        for base in range(0, order, 4):
            acc = {}

            def add(key, value):
                acc[key] = value if key not in acc else acc[key] + value

            for m in range(order):
                chan = [
                    [chan_ref[t, r, m, pl.ds(g * ROWS, ROWS), :] for g in range(groups)]
                    for r in range(2)
                ]
                for l in range(base, base + 4):
                    inv_re = row(t, min(l, m), max(l, m))
                    inv_im = row(t, max(l, m), min(l, m)) if l != m else None
                    if l > m:
                        inv_im = -inv_im
                    for g in range(groups):
                        re, im = chan[0][g], chan[1][g]
                        if inv_im is None:
                            add((l, 0, g), re * inv_re)
                            add((l, 1, g), -(im * inv_re))
                        else:
                            add((l, 0, g), re * inv_re + im * inv_im)
                            add((l, 1, g), re * inv_im - im * inv_re)
            for (l, r, g), value in acc.items():
                value = value * scale[t, pl.ds(l, 1), :]
                weight[t, r, l, pl.ds(g * ROWS, ROWS), :] = value.astype(jnp.bfloat16).astype(
                    jnp.float32
                )

    def precode(k, carry):
        for t in range(tiles):
            acc = {}
            for l in range(order):
                w_re = [weight[t, 0, l, pl.ds(g * ROWS, ROWS), :] for g in range(groups)]
                w_im = [weight[t, 1, l, pl.ds(g * ROWS, ROWS), :] for g in range(groups)]
                for s in range(syms):
                    s_re = sym_ref[t, k, pl.ds((l * 2 + 0) * syms + s, 1), :]
                    s_im = sym_ref[t, k, pl.ds((l * 2 + 1) * syms + s, 1), :]
                    for g in range(groups):
                        re = w_re[g] * s_re - w_im[g] * s_im
                        im = w_re[g] * s_im + w_im[g] * s_re
                        if l == 0:
                            acc[s, g] = (re, im)
                        else:
                            old = acc[s, g]
                            acc[s, g] = (old[0] + re, old[1] + im)
            for r in range(2):
                whole = jnp.concatenate(
                    [acc[s, g][r] for s in range(syms) for g in range(groups)], axis=0
                )
                high = whole.astype(jnp.bfloat16)
                spot = pl.ds((r * tiles + t) * WIDE, WIDE)
                grid_high[k, :, spot] = high
                grid_rest[k, :, spot] = (whole - high.astype(jnp.float32)).astype(jnp.bfloat16)
        return carry

    lax.fori_loop(0, per_block, precode, 0)

    quarter = NFFT // 4
    height = syms * antennas

    def transform(n, carry):
        high = grid_high[...].reshape(per_block * height, 2 * tiles * WIDE)
        rest = grid_rest[...].reshape(per_block * height, 2 * tiles * WIDE)
        spec[...] = (
            jnp.dot(high, high_ref[n], preferred_element_type=jnp.float32)
            + jnp.dot(rest, high_ref[n], preferred_element_type=jnp.float32)
            + jnp.dot(high, rest_ref[n], preferred_element_type=jnp.float32)
        )
        for s in range(syms):
            for g in range(groups):
                part = [None] * 4
                for k in range(per_block):
                    rows = pl.ds(k * height + s * antennas + g * ROWS, ROWS)
                    re = spec[rows, pl.ds(0, WIDE)]
                    im = spec[rows, pl.ds(WIDE, WIDE)]
                    if k > 0:
                        cos = twist_ref[n, pl.ds(2 * k, 1), :]
                        sin = twist_ref[n, pl.ds(2 * k + 1, 1), :]
                        re, im = re * cos - im * sin, re * sin + im * cos
                    old = part[k % 4]
                    part[k % 4] = (re, im) if old is None else (old[0] + re, old[1] + im)
                (r0, i0), (r1, i1), (r2, i2), (r3, i3) = part
                even_re, even_im, odd_re, odd_im = r0 + r2, i0 + i2, r1 + r3, i1 + i3
                gap_re, gap_im, far_re, far_im = r0 - r2, i0 - i2, r1 - r3, i1 - i3
                outs = (
                    (even_re + odd_re, even_im + odd_im),
                    (gap_re - far_im, gap_im + far_re),
                    (even_re - odd_re, even_im - odd_im),
                    (gap_re + far_im, gap_im - far_re),
                )
                for q, pair in enumerate(outs):
                    spot = pl.ds(pl.multiple_of(q * quarter + n * WIDE, WIDE), WIDE)
                    for r in range(2):
                        out_ref[r, s, pl.ds(g * ROWS, ROWS), spot] = pair[r]
        return carry

    lax.fori_loop(0, quarter // WIDE, transform, 0)


def transform_tables(blocks, subcarriers):
    sub = subcarriers // blocks
    quarter = NFFT // 4
    p = np.arange(blocks)[:, None]
    n = np.arange(quarter)[None, :]
    angle = 2.0 * np.pi / NFFT * ((sub * p - subcarriers // 2) * n % NFFT)
    cos = np.cos(angle) / math.sqrt(NFFT)
    sin = np.sin(angle) / math.sqrt(NFFT)
    count = quarter // WIDE
    real = np.concatenate([cos, -sin], 0).reshape(2 * blocks, count, 1, WIDE)
    imag = np.concatenate([sin, cos], 0).reshape(2 * blocks, count, 1, WIDE)
    table = np.concatenate([real, imag], 2).transpose(1, 0, 2, 3)
    table = table.reshape(count, 2 * blocks, 2 * WIDE).astype(np.float32)
    high = table.astype(jnp.bfloat16)
    rest = (table - high.astype(np.float32)).astype(jnp.bfloat16)
    turns = 2.0 * np.pi / NFFT * (np.arange(sub)[:, None] * n)
    twist = np.stack([np.cos(turns), np.sin(turns)], 1).astype(np.float32)
    twist = twist.reshape(2 * sub, count, WIDE).transpose(1, 0, 2)
    return high, rest, np.ascontiguousarray(twist)


def reorder_table(sub):
    source = np.arange(sub * WIDE)
    table = np.zeros((sub * WIDE, sub * WIDE), np.float32)
    table[source, (source % sub) * WIDE + source // sub] = 1.0
    return table.astype(jnp.bfloat16)


def per_device(channel, symbols, layers, user_ids, user_power, neighbours, coupling):
    lanes = lax.axis_size("lane")
    cells = lax.axis_size("cell")
    _, antennas, _, order, blocks = channel.shape
    syms, subcarriers = symbols.shape[3:]
    sub = subcarriers // blocks
    chunk = blocks // lanes
    tiles = blocks // WIDE
    quarter = NFFT // 4
    f32 = jnp.float32
    high, rest, twist = transform_tables(blocks, subcarriers)
    chan = channel[0]

    amp, own = pl.pallas_call(
        functools.partial(power_kernel, chunk=chunk),
        out_shape=(
            jax.ShapeDtypeStruct((order, blocks), f32),
            jax.ShapeDtypeStruct((1, WIDE), f32),
        ),
        in_specs=[VMEM] * 3,
        out_specs=(VMEM, VMEM),
        name="power",
    )(layers, user_ids[0], user_power)
    transmit = lax.all_to_all(jnp.broadcast_to(own, (cells, WIDE)), "cell", 0, 0, tiled=True)

    parts = pl.pallas_call(
        functools.partial(gram_kernel, chunk=chunk),
        out_shape=jax.ShapeDtypeStruct((lanes, order * ROWS, WIDE), f32),
        in_specs=[VMEM] * 2,
        out_specs=VMEM,
        compiler_params=params(16),
        name="gram",
    )(chan, layers)
    parts = lax.all_to_all(parts, "lane", 0, 0, tiled=True)

    sym, turned = pl.pallas_call(
        arrange_kernel,
        out_shape=(
            jax.ShapeDtypeStruct((tiles, sub, order * 2 * syms, WIDE), f32),
            jax.ShapeDtypeStruct((tiles, 2, order, antennas, WIDE), f32),
        ),
        in_specs=[VMEM] * 3,
        out_specs=(VMEM, VMEM),
        scratch_shapes=[pltpu.VMEM((tiles, antennas * 2 * order, WIDE), f32)],
        compiler_params=params(24),
        cost_estimate=pl.CostEstimate(flops=10**9, bytes_accessed=8 * 10**6, transcendentals=0),
        name="arrange",
    )(symbols.reshape(order * 2 * syms, subcarriers), jnp.asarray(reorder_table(sub)), chan)

    packs = pl.pallas_call(
        solve_kernel,
        out_shape=jax.ShapeDtypeStruct((lanes, order * ROWS + ROWS, WIDE), f32),
        in_specs=[SMEM, SMEM, VMEM, VMEM],
        out_specs=VMEM,
        scratch_shapes=[pltpu.VMEM((order * order, WIDE), f32)] * 8,
        compiler_params=params(16),
        name="solve",
    )(neighbours, coupling, parts, transmit)
    packs = lax.all_to_all(packs, "lane", 0, 0, tiled=True)

    out = pl.pallas_call(
        functools.partial(transmit_kernel, chunk=chunk),
        out_shape=jax.ShapeDtypeStruct((2, syms, antennas, NFFT), f32),
        in_specs=[VMEM] * 7,
        out_specs=VMEM,
        scratch_shapes=[
            pltpu.VMEM((tiles, order * order, WIDE), f32),
            pltpu.VMEM((tiles, order, WIDE), f32),
            pltpu.VMEM((tiles, 2, order, antennas, WIDE), f32),
            pltpu.VMEM((sub, syms * antennas, 2 * tiles * WIDE), jnp.bfloat16),
            pltpu.VMEM((sub, syms * antennas, 2 * tiles * WIDE), jnp.bfloat16),
            pltpu.VMEM((sub * syms * antennas, 2 * WIDE), f32),
        ],
        compiler_params=params(32),
        name="transmit",
    )(packs, amp, turned, sym, jnp.asarray(high), jnp.asarray(rest), jnp.asarray(twist))
    return jnp.transpose(out, (2, 0, 1, 3))[None]


def solution(mesh):
    in_specs = (
        P("cell", "lane", None, None, None),
        P("cell", None, None, None, None),
        P("cell", None),
        P("cell", None, None),
        P("cell", None),
        P(),
        P(),
    )
    out_specs = P("cell", "lane", None, None, None)
    return jax.shard_map(
        per_device, mesh=mesh, in_specs=in_specs, out_specs=out_specs, check_vma=False
    )
```

profile of v0, /device:TPU:0, one launch (start us, length us, event | category | flops | bytes accessed | tf_op | source)
XLA Modules:
  0.0 56.2 jit_solution(17298648829153275316)
XLA Ops:
  0.0 1.5 %power.1 = (f32[16,256]{1,0:T(8,128)}, f32[1,128]{1,0:T(1,128)}) custom-call(s32[1,256]{1,0:T(1,128)} %layers_ref.3, s32[16,256]{1,0:T(8,128)} %bitcast.11, f32[1,128]{1,0:T(1,128)} %power_ref.1), custom_call_target="tpu_custom_call" | custom-call | tf_op jit(solution)/shard_map/power/pallas_call | solution.py:483
  1.5 1.2 %broadcast_in_dim.8 = f32[8,1,128]{2,1,0:T(1,128)} broadcast(f32[128]{0:T(128)} %bitcast.12), dimensions={2} | broadcast | bytes 4608 | tf_op jit(solution)/shard_map/broadcast_in_dim | solution.py:493
  2.7 5.2 %all-to-all-start.1 = ((f32[8,1,128]{2,1,0:T(1,128)}), f32[8,1,128]{2,1,0:T(1,128)S(1)}, u32[]{:S(2)}, u32[]{:S(2)}) async-start(f32[8,1,128]{2,1,0:T(1,128)} %broadcast_in_dim.8), calls=%async_computation.1 | async-start | bytes 8192 | tf_op jit(solution)/shard_map/all_to_all | solution.py:493
  7.8 0.0 copy-start.3
  7.8 1.0 %copy-done.3 = f32[1,16,2,16,256]{4,3,2,1,0:T(8,128)S(1)} copy-done((f32[1,16,2,16,256]{4,3,2,1,0:T(8,128)S(1)}, f32[1,16,2,16,256]{4,3,2,1,0:T(8,128)}, u32[]{:S(2)}) %copy-start.3) | copy-done | bytes 524312
  8.9 0.0 copy-start.13
  8.9 0.7 %copy-done.13 = s32[1,256]{1,0:T(1,128)S(1)} copy-done((s32[1,256]{1,0:T(1,128)S(1)}, s32[1,256]{1,0:T(1,128)}, u32[]{:S(2)}) %copy-start.13) | copy-done | bytes 1048
  9.5 0.0 copy-start.14
  9.6 0.0 copy-start.4
  9.6 1.3 %gram.1 = f32[4,128,128]{2,1,0:T(8,128)S(1)} custom-call(f32[16,2,16,256]{3,2,1,0:T(8,128)S(1)} %bitcast.8, s32[1,256]{1,0:T(1,128)S(1)} %copy-done.13), custom_call_target="tpu_custom_call" | custom-call | tf_op jit(solution)/shard_map/gram/pallas_call | solution.py:495
  10.8 1.6 %all-to-all-done.1 = f32[8,1,128]{2,1,0:T(1,128)S(1)} async-done(((f32[8,1,128]{2,1,0:T(1,128)}), f32[8,1,128]{2,1,0:T(1,128)S(1)}, u32[]{:S(2)}, u32[]{:S(2)}) %all-to-all-start.1) | async-done | bytes 4128 | tf_op jit(solution)/shard_map/all_to_all | solution.py:493
  12.4 13.5 %all_to_all.18.parts_ref = f32[4,128,128]{2,1,0:T(8,128)S(1)} all-to-all(f32[4,128,128]{2,1,0:T(8,128)S(1)} %gram.1), channel_id=1, replica_groups=mesh['cell'=8,'lane'=4] {'lane'}, dimensions={0} | all-to-all | bytes 524288 | tf_op jit(solution)/shard_map/all_to_all | solution.py:503
  25.9 0.0 copy-start.11
  25.9 0.7 %copy-done.11 = s32[8,6]{1,0:T(8,128)S(1)} copy-done((s32[8,6]{1,0:T(8,128)S(1)}, s32[8,6]{1,0:T(8,128)}, u32[]{:S(2)}) %copy-start.11) | copy-done | bytes 216
  26.6 0.0 copy-start.12
  26.6 0.7 %copy-done.12 = f32[8,6]{1,0:T(8,128)S(1)} copy-done((f32[8,6]{1,0:T(8,128)S(1)}, f32[8,6]{1,0:T(8,128)}, u32[]{:S(2)}) %copy-start.12) | copy-done | bytes 216
  27.3 4.5 %solve.1 = f32[4,136,128]{2,1,0:T(8,128)} custom-call(s32[8,6]{1,0:T(8,128)S(1)} %copy-done.11, f32[8,6]{1,0:T(8,128)S(1)} %copy-done.12, f32[4,128,128]{2,1,0:T(8,128)S(1)} %all_to_all.18.parts_ref, f32[8,128]{1,0:T(8,128)S(1)} %bitcast.10), custom_call_target="tpu_custom_call" | custom-call | tf_op jit(solution)/shard_map/solve/pallas_call | solution.py:519
  31.8 3.4 %all-to-all-start.2 = ((f32[4,136,128]{2,1,0:T(8,128)}), f32[4,136,128]{2,1,0:T(8,128)S(1)}, u32[]{:S(2)}, u32[]{:S(2)}) async-start(f32[4,136,128]{2,1,0:T(8,128)} %solve.1), calls=%async_computation.2 | async-start | bytes 557056 | tf_op jit(solution)/shard_map/all_to_all | solution.py:528
  35.3 0.0 copy-done.14
  35.3 0.1 reshape.9.symbols_ref
  35.5 0.0 copy-done.4
  35.5 0.0 copy-start
  35.5 2.3 %copy-done = bf16[1536,1536]{1,0:T(8,128)(2,1)S(1)} copy-done((bf16[1536,1536]{1,0:T(8,128)(2,1)S(1)}, bf16[1536,1536]{1,0:T(8,128)(2,1)}, u32[]{:S(2)}) %copy-start) | copy-done | bytes 4718616
  37.8 0.0 copy-start.1
  37.8 0.0 copy-start.9
  37.8 0.0 copy-start.10
  37.8 2.0 %arrange.1 = (f32[2,12,64,128]{3,2,1,0:T(8,128)S(1)}, f32[2,2,16,16,128]{4,3,2,1,0:T(8,128)S(1)}) custom-call(bf16[64,3072]{1,0:T(8,128)(2,1)S(1)} %reshape.9.symbols_ref, bf16[1536,1536]{1,0:T(8,128)(2,1)S(1)} %copy-done, f32[16,2,16,256]{3,2,1,0:T(8,128)S(1)} %bitcast.9), custom_call_target="tpu_custom_call" | custom-call | flops 1000000000 | bytes 8000000 | tf_op jit(solution)/shard_map/arrange/pallas_call | solution.py:505
  39.8 0.0 copy-start.5
  39.8 0.9 %copy-done.5 = f32[2,12,64,128]{3,2,1,0:T(8,128)} copy-done((f32[2,12,64,128]{3,2,1,0:T(8,128)}, f32[2,12,64,128]{3,2,1,0:T(8,128)S(1)}, u32[]{:S(2)}) %copy-start.5) | copy-done | bytes 786456
  40.7 0.0 copy-start.7
  40.7 0.8 %copy-done.7 = f32[2,2,16,16,128]{4,3,2,1,0:T(8,128)} copy-done((f32[2,2,16,16,128]{4,3,2,1,0:T(8,128)}, f32[2,2,16,16,128]{4,3,2,1,0:T(8,128)S(1)}, u32[]{:S(2)}) %copy-start.7) | copy-done | bytes 524312
  41.5 2.0 %all-to-all-done.2.packs_ref = f32[4,136,128]{2,1,0:T(8,128)S(1)} async-done(((f32[4,136,128]{2,1,0:T(8,128)}), f32[4,136,128]{2,1,0:T(8,128)S(1)}, u32[]{:S(2)}, u32[]{:S(2)}) %all-to-all-start.2) | async-done | bytes 278560 | tf_op jit(solution)/shard_map/all_to_all | solution.py:528
  43.5 0.0 copy-done.1
  43.5 0.0 copy-done.9
  43.5 0.0 copy-done.10
  43.5 0.0 copy-start.2
  43.5 1.6 %copy-done.2 = bf16[8,512,256]{2,1,0:T(8,128)(2,1)S(1)} copy-done((bf16[8,512,256]{2,1,0:T(8,128)(2,1)S(1)}, bf16[8,512,256]{2,1,0:T(8,128)(2,1)}, u32[]{:S(2)}) %copy-start.2) | copy-done | bytes 2097176
  45.1 0.0 copy-start.6
  45.1 1.1 %copy-done.6 = f32[2,12,64,128]{3,2,1,0:T(8,128)S(1)} copy-done((f32[2,12,64,128]{3,2,1,0:T(8,128)S(1)}, f32[2,12,64,128]{3,2,1,0:T(8,128)}, u32[]{:S(2)}) %copy-start.6) | copy-done | bytes 786456
  46.2 0.0 copy-start.8
  46.2 1.0 %copy-done.8 = f32[2,2,16,16,128]{4,3,2,1,0:T(8,128)S(1)} copy-done((f32[2,2,16,16,128]{4,3,2,1,0:T(8,128)S(1)}, f32[2,2,16,16,128]{4,3,2,1,0:T(8,128)}, u32[]{:S(2)}) %copy-start.8) | copy-done | bytes 524312
  47.3 7.1 %transmit.1 = f32[2,2,16,4096]{3,2,1,0:T(8,128)S(1)} custom-call(f32[4,136,128]{2,1,0:T(8,128)S(1)} %all-to-all-done.2.packs_ref, f32[16,256]{1,0:T(8,128)S(1)} %copy-done.10, f32[2,2,16,16,128]{4,3,2,1,0:T(8,128)S(1)} %copy-done.8, f32[2,12,64,128]{3,2,1,0:T(8,128)S(1)} %copy-done.6, bf16[8,512,256]{2,1,0:T(8,128)(2,1)S(1)} %copy-done.2, ...), custom_call_target="tpu_custom_call" | custom-call | tf_op jit(solution)/shard_map/transmit/pallas_call | solution.py:530
  54.4 1.8 %copy.13 = f32[1,16,2,2,4096]{4,3,2,1,0:T(2,128)} copy(f32[1,16,2,2,4096]{4,1,3,2,0:T(8,128)S(1)} %bitcast.7) | data formatting | bytes 2097152 | tf_op jit(solution)/shard_map/broadcast_in_dim | solution.py:546
Async XLA Ops:
  2.7 9.8 %all-to-all-start.1 = ((f32[8,1,128]{2,1,0:T(1,128)}), f32[8,1,128]{2,1,0:T(1,128)S(1)}, u32[]{:S(2)}, u32[]{:S(2)}) async-start(f32[8,1,128]{2,1,0:T(1,128)} %broadcast_in_dim.8), calls=%async_computation.1 | async-start | bytes 8192 | tf_op jit(solution)/shard_map/all_to_all | solution.py:493
  7.8 1.0 %copy-start.3 = (f32[1,16,2,16,256]{4,3,2,1,0:T(8,128)S(1)}, f32[1,16,2,16,256]{4,3,2,1,0:T(8,128)}, u32[]{:S(2)}) copy-start(f32[1,16,2,16,256]{4,3,2,1,0:T(8,128)} %param.11) | copy-start | bytes 1572868
  8.9 0.7 %copy-start.13 = (s32[1,256]{1,0:T(1,128)S(1)}, s32[1,256]{1,0:T(1,128)}, u32[]{:S(2)}) copy-start(s32[1,256]{1,0:T(1,128)} %layers_ref.3) | copy-start | bytes 3076
  9.5 25.7 %copy-start.14 = (bf16[1,16,2,2,3072]{4,3,2,1,0:T(2,128)(2,1)S(1)}, bf16[1,16,2,2,3072]{4,3,2,1,0:T(2,128)(2,1)}, u32[]{:S(2)}) copy-start(bf16[1,16,2,2,3072]{4,3,2,1,0:T(2,128)(2,1)} %param.12) | copy-start | bytes 1179652
  9.6 25.9 %copy-start.4 = (f32[1,16,2,16,256]{4,3,2,1,0:T(8,128)S(1)}, f32[1,16,2,16,256]{4,3,2,1,0:T(8,128)}, u32[]{:S(2)}) copy-start(f32[1,16,2,16,256]{4,3,2,1,0:T(8,128)} %param.11) | copy-start | bytes 1572868
  25.9 0.7 %copy-start.11 = (s32[8,6]{1,0:T(8,128)S(1)}, s32[8,6]{1,0:T(8,128)}, u32[]{:S(2)}) copy-start(s32[8,6]{1,0:T(8,128)} %neigh_ref.1) | copy-start | bytes 580
  26.6 0.7 %copy-start.12 = (f32[8,6]{1,0:T(8,128)S(1)}, f32[8,6]{1,0:T(8,128)}, u32[]{:S(2)}) copy-start(f32[8,6]{1,0:T(8,128)} %coup_ref.1) | copy-start | bytes 580
  31.8 11.6 %all-to-all-start.2 = ((f32[4,136,128]{2,1,0:T(8,128)}), f32[4,136,128]{2,1,0:T(8,128)S(1)}, u32[]{:S(2)}, u32[]{:S(2)}) async-start(f32[4,136,128]{2,1,0:T(8,128)} %solve.1), calls=%async_computation.2 | async-start | bytes 557056 | tf_op jit(solution)/shard_map/all_to_all | solution.py:528
  35.5 2.3 %copy-start = (bf16[1536,1536]{1,0:T(8,128)(2,1)S(1)}, bf16[1536,1536]{1,0:T(8,128)(2,1)}, u32[]{:S(2)}) copy-start(bf16[1536,1536]{1,0:T(8,128)(2,1)} %constant.8.clone.order_ref) | copy-start | bytes 14155780
  37.8 5.7 %copy-start.1 = (bf16[8,512,256]{2,1,0:T(8,128)(2,1)S(1)}, bf16[8,512,256]{2,1,0:T(8,128)(2,1)}, u32[]{:S(2)}) copy-start(bf16[8,512,256]{2,1,0:T(8,128)(2,1)} %constant.10.clone.rest_ref) | copy-start | bytes 6291460
  37.8 5.7 %copy-start.9 = (f32[8,24,128]{2,1,0:T(8,128)S(1)}, f32[8,24,128]{2,1,0:T(8,128)}, u32[]{:S(2)}) copy-start(f32[8,24,128]{2,1,0:T(8,128)} %constant.11.clone.twist_ref) | copy-start | bytes 294916
  37.8 5.7 %copy-start.10 = (f32[16,256]{1,0:T(8,128)S(1)}, f32[16,256]{1,0:T(8,128)}, u32[]{:S(2)}) copy-start(f32[16,256]{1,0:T(8,128)} %get-tuple-element.10.amp_ref) | copy-start | bytes 49156
  39.8 0.9 %copy-start.5 = (f32[2,12,64,128]{3,2,1,0:T(8,128)}, f32[2,12,64,128]{3,2,1,0:T(8,128)S(1)}, u32[]{:S(2)}) copy-start(f32[2,12,64,128]{3,2,1,0:T(8,128)S(1)} %get-tuple-element.12.sym_ref) | copy-start | bytes 2359300
  40.7 0.8 %copy-start.7 = (f32[2,2,16,16,128]{4,3,2,1,0:T(8,128)}, f32[2,2,16,16,128]{4,3,2,1,0:T(8,128)S(1)}, u32[]{:S(2)}) copy-start(f32[2,2,16,16,128]{4,3,2,1,0:T(8,128)S(1)} %get-tuple-element.11.chan_ref) | copy-start | bytes 1572868
  43.5 1.6 %copy-start.2 = (bf16[8,512,256]{2,1,0:T(8,128)(2,1)S(1)}, bf16[8,512,256]{2,1,0:T(8,128)(2,1)}, u32[]{:S(2)}) copy-start(bf16[8,512,256]{2,1,0:T(8,128)(2,1)} %constant.9.clone.high_ref) | copy-start | bytes 6291460
  45.1 1.1 %copy-start.6 = (f32[2,12,64,128]{3,2,1,0:T(8,128)S(1)}, f32[2,12,64,128]{3,2,1,0:T(8,128)}, u32[]{:S(2)}) copy-start(f32[2,12,64,128]{3,2,1,0:T(8,128)} %copy-done.5) | copy-start | bytes 2359300
  46.2 1.0 %copy-start.8 = (f32[2,2,16,16,128]{4,3,2,1,0:T(8,128)S(1)}, f32[2,2,16,16,128]{4,3,2,1,0:T(8,128)}, u32[]{:S(2)}) copy-start(f32[2,2,16,16,128]{4,3,2,1,0:T(8,128)} %copy-done.7) | copy-start | bytes 1572868
where the time goes:
time: 56.8 us; the launch traced here: 56.2 us
  Pallas kernels  16.4 us (29%)
  local copies, waits for them, and re-layouts  14 us (25%)
  blocking collectives  13.5 us (24%)
  starting transfers between devices  8.62 us (15%)
  waiting for transfers between devices  3.59 us (6%)
    all_to_all x1, blocking collectives, per_device(): parts = lax.all_to_all(parts, 'lane', 0, 0, tiled=True)  13.5 us
    unnamed x30, local copies, waits for them, and re-layouts  10.9 us
    pallas_call x1, Pallas kernels, per_device(): pl.pallas_call(functools.partial(transmit_kernel, chunk=chunk), out_shape...  7.11 us
    all_to_all x1, starting transfers between devices, per_device(): lax.all_to_all(jnp.broadcast_to(own, (cells, WIDE)), 'cell', 0, 0, tiled=...  5.17 us
    pallas_call x1, Pallas kernels, per_device(): pl.pallas_call(solve_kernel, out_shape=jax.ShapeDtypeStruct((lanes, order...  4.54 us
    all_to_all x1, starting transfers between devices, per_device(): packs = lax.all_to_all(packs, 'lane', 0, 0, tiled=True)  3.45 us
    all_to_all x1, waiting for transfers between devices, per_device(): packs = lax.all_to_all(packs, 'lane', 0, 0, tiled=True)  2 us
    pallas_call x1, Pallas kernels, per_device(): pl.pallas_call(arrange_kernel, out_shape=(jax.ShapeDtypeStruct((tiles, su...  1.98 us
  transfers between devices with their start and end apart: 2, of which 2 were waited for; matrix products, arithmetic and copies ran while one was open for 0% of the time, Pallas kernels for 6%

commit v1 on v0

v1 whole, which is shorter than its diff:
```python
import functools
import math

import jax
import jax.numpy as jnp
import numpy as np
from jax import lax
from jax.experimental import pallas as pl
from jax.experimental.pallas import tpu as pltpu
from jax.sharding import PartitionSpec as P

NFFT = 4096
NS_STEPS = 6
NORM_EPS = 1e-06
NOISE_FLOOR = 0.05
WIDE = 128
HALF = WIDE // 2
ROWS = 8

VMEM = pl.BlockSpec(memory_space=pltpu.VMEM)
HBM = pl.BlockSpec(memory_space=pltpu.HBM)


def lane_iota():
    return lax.broadcasted_iota(jnp.int32, (ROWS, WIDE), 1)


def row_iota():
    return lax.broadcasted_iota(jnp.int32, (ROWS, WIDE), 0)


def turn(value, shift):
    shift = shift % WIDE
    return value if shift == 0 else pltpu.roll(value, shift, 1)


def params(mib):
    return pltpu.CompilerParams(vmem_limit_bytes=mib * 1024 * 1024)


def gram_kernel(*refs, lanes, chunk):
    ins, outs = refs[:6], refs[10 : 10 + lanes]
    amp_all, own, mix, turned = refs[6:10]
    channel, layers, ids_all, power, neigh, coup, pieces, stage, sems = refs[10 + lanes :]
    antennas, _, order, blocks = channel.shape
    users = power.shape[1]
    tiles = blocks // WIDE
    small = [
        pltpu.make_async_copy(src, dst, sems.at[i])
        for i, (src, dst) in enumerate(
            (
                (ins[1], layers),
                (ins[2].at[0], ids_all),
                (ins[3], power),
                (ins[4], neigh),
                (ins[5], coup),
            )
        )
    ]
    large = [
        pltpu.make_async_copy(
            ins[0].at[0, :, :, :, pl.ds(t * WIDE, WIDE)],
            channel.at[:, :, :, pl.ds(t * WIDE, WIDE)],
            sems.at[5 + t],
        )
        for t in range(tiles)
    ]
    for copy in small + large:
        copy.start()
    for copy in small:
        copy.wait()

    rooted = jnp.sqrt(power[...])
    sums = []
    for t in range(tiles):
        spot = pl.ds(t * WIDE, WIDE)
        granted = layers[:, spot]
        total = jnp.zeros((ROWS, WIDE), jnp.float32)
        for h in range(order // ROWS):
            ids = ids_all[pl.ds(h * ROWS, ROWS), spot]
            picked = jnp.zeros((ROWS, WIDE), jnp.float32)
            for u in range(users // WIDE):
                table = jnp.broadcast_to(rooted[:, u * WIDE : (u + 1) * WIDE], (ROWS, WIDE))
                found = jnp.take_along_axis(table, ids % WIDE, axis=1, mode="promise_in_bounds")
                picked = jnp.where(ids // WIDE == u, found, picked)
            amp = jnp.where(row_iota() + h * ROWS < granted, picked, 0.0)
            amp_all[t, pl.ds(h * ROWS, ROWS), :] = amp
            total = total + amp * amp
        sums.append(jnp.sum(total, axis=0, keepdims=True) / order)
    lane = lax.axis_index("lane")
    start = lane * chunk
    mine = jnp.broadcast_to(sums[0], (ROWS, WIDE))
    for t in range(1, tiles):
        mine = jnp.where(start // WIDE == t, jnp.broadcast_to(sums[t], (ROWS, WIDE)), mine)
    mine = pltpu.roll(mine, lax.rem(WIDE - lax.rem(start, WIDE), WIDE), 1)
    both = jnp.where(lane_iota() < HALF, mine, pltpu.roll(mine, HALF, 1))
    own[...] = jnp.broadcast_to(both[0:1][None], own.shape)
    cell = lax.axis_index("cell")
    mix[...] = jnp.zeros(mix.shape, jnp.float32)
    for k in range(neigh.shape[1]):
        spot = neigh[cell, k]
        mix[spot] = mix[spot] + coup[cell, k]
    low = lane_iota() < HALF
    rows = row_iota()
    for t in range(tiles):
        spot = pl.ds(t * WIDE, WIDE)
        granted = layers[:, spot]
        inside = [rows + h * ROWS < granted for h in range(2)]
        large[t].wait()
        for base in range(0, ROWS, 2):
            tops = (base, base + 1)
            acc = {}

            def add(key, value):
                acc[key] = value if key not in acc else acc[key] + value

            for a in range(antennas):
                re = [channel[a, 0, pl.ds(h * ROWS, ROWS), spot] for h in range(2)]
                im = [channel[a, 1, pl.ds(h * ROWS, ROWS), spot] for h in range(2)]
                for l in tops:
                    lre = channel[a, 0, pl.ds(l, 1), spot]
                    lim = channel[a, 1, pl.ds(l, 1), spot]
                    add((l, "re", 0), lre * re[0] + lim * im[0])
                    add((l, "re", 1), lre * re[1] + lim * im[1])
                    add((l, "im", 0), lim * re[0] - lre * im[0])
                    g = l + ROWS
                    gre = channel[a, 0, pl.ds(g, 1), spot]
                    gim = channel[a, 1, pl.ds(g, 1), spot]
                    add((g, "re", 1), gre * re[1] + gim * im[1])
                    add((g, "im", 0), gim * re[0] - gre * im[0])
                    add((g, "im", 1), gim * re[1] - gre * im[1])
            for l in tops:
                g = l + ROWS
                here = granted > l
                there = granted > g
                upper = [
                    jnp.where(rows >= l, acc[l, "re", 0], acc[l, "im", 0]),
                    acc[l, "re", 1],
                ]
                lower = [
                    acc[g, "im", 0],
                    jnp.where(rows >= l, acc[g, "re", 1], acc[g, "im", 1]),
                ]
                for h in range(2):
                    top = jnp.where(jnp.logical_and(inside[h], here), upper[h], 0.0)
                    bottom = jnp.where(jnp.logical_and(inside[h], there), lower[h], 0.0)
                    for z in range(t * WIDE // chunk, (t + 1) * WIDE // chunk):
                        off = z * chunk - t * WIDE
                        where = pl.ds(l * 2 * ROWS + h * ROWS, ROWS)
                        pieces[lane ^ z, where, :] = jnp.where(
                            low, turn(top, -off), turn(bottom, HALF - off)
                        )
    for s in range(lanes):
        outs[s][...] = pieces[s]
    for t in range(tiles):
        for a in range(antennas):
            for r in range(2):
                for h in range(order // ROWS):
                    stage[t, pl.ds((a * 2 + r) * order + h * ROWS, ROWS), :] = channel[
                        a, r, pl.ds(h * ROWS, ROWS), pl.ds(t * WIDE, WIDE)
                    ]
        for r in range(2):
            for m in range(order):
                for h in range(antennas // ROWS):
                    first = h * ROWS * 2 * order + r * order + m
                    turned[t, r, m, pl.ds(h * ROWS, ROWS), :] = stage[
                        t, pl.ds(first, ROWS, stride=2 * order), :
                    ]


def solve_kernel(*refs, lanes):
    trans, mix = refs[:2]
    parts, out = refs[2 : 2 + lanes], refs[3 + lanes]
    pack, gram, e_a, e_b, s_a, s_b, d_re, d_im = refs[4 + lanes :]
    order = 2 * ROWS
    low = lane_iota() < HALF
    rows = row_iota()
    sign = jnp.where(low, -1.0, 1.0)

    def at(l, h):
        return pl.ds(l * order + h * ROWS, ROWS)

    def column(l, h):
        return pl.ds(h * ROWS * order + l, ROWS, stride=order)

    def row(ref, l, k):
        return ref[pl.ds(l * order + k, 1), :]

    for l in range(ROWS):
        for h in range(2):
            value = parts[0][at(l, h), :]
            for s in range(1, lanes):
                value = value + parts[s][at(l, h), :]
            other = pltpu.roll(value, HALF, 1)
            pack[at(l, h), :] = jnp.where(low, value, other)
            pack[at(l + ROWS, h), :] = jnp.where(low, other, value)

    sigma = jnp.full((1, WIDE), NOISE_FLOOR, jnp.float32)
    for c in range(trans.shape[0]):
        sigma = sigma + mix[c] * trans[c]

    trace = order * sigma
    for l in range(order):
        trace = trace + row(pack, l, l)
    inverse = 1.0 / trace
    kept = 1.0 - sigma * inverse

    for l in range(order):
        for h in range(2):
            here = pack[at(l, h), :]
            across = pack[column(l, h), :]
            above = jnp.where(low, here, -across)
            below = jnp.where(low, across, here)
            if h * ROWS > l:
                value = above
            elif h * ROWS + ROWS - 1 < l:
                value = below
            else:
                value = jnp.where(rows + h * ROWS >= l, above, below)
                value = jnp.where(jnp.logical_and(rows + h * ROWS == l, ~low), 0.0, value)
            gram[at(l, h), :] = value
            error = -value * inverse
            total = error
            if h * ROWS <= l < h * ROWS + ROWS:
                spot = jnp.logical_and(rows + h * ROWS == l, low)
                error = error + jnp.where(spot, kept, 0.0)
                total = error + jnp.where(spot, 1.0, 0.0)
            e_a[at(l, h), :] = error
            s_a[at(l, h), :] = total

    def spread(ref):
        for l in range(order):
            for h in range(2):
                value = ref[at(l, h), :]
                other = pltpu.roll(value, HALF, 1)
                d_re[at(l, h), :] = jnp.where(low, value, other)
                d_im[at(l, h), :] = jnp.where(low, other, value)

    def products(jobs):
        for base in range(0, order, 2):
            halves = (0, 1) if base < ROWS else (1,)
            plain, crossed = {}, {}
            for l in (base, base + 1):
                for j, (_, _, start) in enumerate(jobs):
                    for h in halves:
                        if start is not None:
                            plain[l, j, h] = start[at(l, h), :]
            for k in range(order):
                right = {
                    (j, h): ref[at(k, h), :] for j, (ref, _, _) in enumerate(jobs) for h in halves
                }
                for l in (base, base + 1):
                    left_re = row(d_re, l, k)
                    left_im = row(d_im, l, k) if k != l else None
                    for (j, h), value in right.items():
                        key = (l, j, h)
                        term = left_re * value
                        plain[key] = plain[key] + term if key in plain else term
                        if left_im is not None:
                            term = left_im * value
                            crossed[key] = crossed[key] + term if key in crossed else term
            for (l, j, h), value in plain.items():
                cross = pltpu.roll(crossed[l, j, h], HALF, 1)
                jobs[j][1][at(l, h), :] = value + sign * cross
        for _, ref, _ in jobs:
            for l in range(ROWS, order):
                ref[at(l, 0), :] = -sign * ref[column(l, 0), :]

    spread(e_a)
    products([(e_a, e_b, None)])

    def two_steps(_, carry):
        spread(e_b)
        products([(e_b, e_a, None), (s_a, s_b, s_a)])
        spread(e_a)
        products([(e_a, e_b, None), (s_b, s_a, s_b)])
        return carry

    lax.fori_loop(0, (NS_STEPS - 2) // 2, two_steps, 0)
    spread(e_b)
    products([(s_a, s_b, s_a)])

    for l in range(order):
        for h in range(2):
            s_a[at(l, h), :] = s_b[at(l, h), :] * inverse
    spread(s_a)
    products([(gram, e_a, None)])

    energy = []
    for h in range(2):
        value = s_a[at(0, h), :] * e_a[at(0, h), :]
        for m in range(1, order):
            value = value + s_a[at(m, h), :] * e_a[at(m, h), :]
        energy.append(value + pltpu.roll(value, HALF, 1))
    last = jnp.where(low, energy[0], energy[1])
    for l in range(ROWS):
        for h in range(2):
            first = s_a[at(l, h), :]
            second = s_a[at(l + ROWS, h), :]
            where = rows + h * ROWS
            value = jnp.where(
                low,
                jnp.where(where >= l, first, pltpu.roll(first, HALF, 1)),
                jnp.where(where >= l + ROWS, pltpu.roll(second, HALF, 1), second),
            )
            out[at(l, h), :] = value
    out[pl.ds(order * ROWS, ROWS), :] = last


def arrange_kernel(far_ref, sym_ref, mark_ref, symbols_ref, sem, flat, stacked, moved):
    copy = pltpu.make_async_copy(far_ref, symbols_ref, sem)
    copy.start()
    copy.wait()
    _, layers, parts, syms, subcarriers = symbols_ref.shape
    tiles, sub, height, _ = sym_ref.shape
    few = 32
    span = sub * few
    quads = WIDE // few
    lanes = lane_iota()
    for l in range(layers):
        for r in range(parts):
            flat[pl.ds((l * parts + r) * syms, syms), :] = symbols_ref[0, l, r].astype(jnp.float32)
    for i in range(tiles * quads):
        stacked[pl.ds(i * height, height), :] = flat[:, pl.ds(i * span, span)].astype(jnp.bfloat16)
    source = lax.broadcasted_iota(jnp.int32, (span, span), 0)
    target = lax.broadcasted_iota(jnp.int32, (span, span), 1)
    table = jnp.where(source == target % few * sub + target // few, 1.0, 0.0).astype(jnp.bfloat16)
    moved[...] = jnp.dot(stacked[...], table, preferred_element_type=jnp.float32)
    for t in range(tiles):
        for k in range(sub):
            for g in range(height // ROWS):
                value = None
                for b in range(quads):
                    rows = pl.ds((t * quads + b) * height + g * ROWS, ROWS)
                    piece = moved[rows, pl.ds(k // quads * WIDE, WIDE)]
                    piece = turn(piece, (b - k % quads) * few)
                    value = piece if b == 0 else jnp.where(lanes >= b * few, piece, value)
                sym_ref[t, k, pl.ds(g * ROWS, ROWS), :] = value
    mark_ref[...] = jnp.zeros(mark_ref.shape, jnp.float32)


def transmit_kernel(*refs, which, last, chunk):
    per_tile = WIDE // chunk
    ins, rest = refs[:per_tile], refs[per_tile:]
    amp, chan, sym, table_ref, twist = rest[:5]
    before = rest[5] if which else None
    out_ref = out = rest[5 + which]
    packs, pack, scale, weight, mixed, grid, table, spec_a, spec_b, sems = rest[
        6 + which : 16 + which
    ]
    if last:
        out, out_sems = rest[16 + which :]
    tiles, _, order, antennas, _ = chan.shape
    per_block, syms = sym.shape[1], sym.shape[2] // (2 * order)
    groups = antennas // ROWS
    lanes = lane_iota()
    lane = lax.axis_index("lane")
    tile = (lane // per_tile) ^ which
    halves = [
        pltpu.make_async_copy(
            table_ref.at[tile], table.at[:, pl.ds(h * 2 * WIDE, 2 * WIDE), :], sems.at[h]
        )
        for h in range(2)
    ]
    for copy in halves:
        copy.start()

    for s, ref in enumerate(ins):
        packs[lane % per_tile ^ s] = ref[...]
    for i in range(2 * ROWS + 1):
        rows = pl.ds(i * ROWS, ROWS)
        value = packs[0, rows, :]
        first, second = value, pltpu.roll(value, HALF, 1)
        for z in range(1, per_tile):
            off = z * chunk
            value = packs[z, rows, :]
            first = jnp.where(lanes >= off, turn(value, off), first)
            second = jnp.where(lanes >= off, turn(value, off - HALF), second)
        if i < 2 * ROWS:
            pack[rows, :] = first
            pack[pl.ds((i + 2 * ROWS) * ROWS, ROWS), :] = second
        else:
            for h, energy in enumerate((first, second)):
                spot = pl.ds(h * ROWS, ROWS)
                scale[spot, :] = amp[tile, spot, :] / jnp.sqrt(energy + NORM_EPS)

    def row(l, m):
        return pack[pl.ds(l * order + m, 1), :]

    for base in range(0, order, 4):
        acc = {}

        def add(key, value):
            acc[key] = value if key not in acc else acc[key] + value

        for m in range(order):
            here = [
                [chan[tile, r, m, pl.ds(g * ROWS, ROWS), :] for g in range(groups)]
                for r in range(2)
            ]
            for l in range(base, base + 4):
                inv_re = row(min(l, m), max(l, m))
                inv_im = row(max(l, m), min(l, m)) if l != m else None
                if l > m:
                    inv_im = -inv_im
                for g in range(groups):
                    re, im = here[0][g], here[1][g]
                    if inv_im is None:
                        add((l, 0, g), re * inv_re)
                        add((l, 1, g), -(im * inv_re))
                    else:
                        add((l, 0, g), re * inv_re + im * inv_im)
                        add((l, 1, g), re * inv_im - im * inv_re)
        for (l, r, g), value in acc.items():
            value = value * scale[pl.ds(l, 1), :]
            weight[r, l, pl.ds(g * ROWS, ROWS), :] = value.astype(jnp.bfloat16).astype(jnp.float32)

    def precode(k, carry):
        acc = {}
        for l in range(order):
            w_re = [weight[0, l, pl.ds(g * ROWS, ROWS), :] for g in range(groups)]
            w_im = [weight[1, l, pl.ds(g * ROWS, ROWS), :] for g in range(groups)]
            for s in range(syms):
                s_re = sym[tile, k, pl.ds((l * 2 + 0) * syms + s, 1), :]
                s_im = sym[tile, k, pl.ds((l * 2 + 1) * syms + s, 1), :]
                for g in range(groups):
                    re = w_re[g] * s_re - w_im[g] * s_im
                    im = w_re[g] * s_im + w_im[g] * s_re
                    if l == 0:
                        acc[s, g] = (re, im)
                    else:
                        old = acc[s, g]
                        acc[s, g] = (old[0] + re, old[1] + im)
        for r in range(2):
            for s in range(syms):
                for g in range(groups):
                    spot = pl.ds(g * ROWS * syms + s, ROWS, stride=syms)
                    mixed[r, spot, :] = acc[s, g][r]
        for r in range(2):
            whole = mixed[r]
            high = whole.astype(jnp.bfloat16)
            grid[k, :, pl.ds(r * WIDE, WIDE)] = high
            grid[k, :, pl.ds((2 + r) * WIDE, WIDE)] = (whole - high.astype(jnp.float32)).astype(
                jnp.bfloat16
            )
        return carry

    lax.fori_loop(0, per_block, precode, 0)

    height = syms * antennas
    count = NFFT // WIDE // 4
    for copy in halves:
        copy.wait()
    left = grid[...].reshape(per_block * height, 4 * WIDE)
    specs = (spec_a, spec_b)

    def product(n):
        specs[n % 2][...] = jnp.dot(left, table[n], preferred_element_type=jnp.float32)

    def combine(n):
        spec = specs[n % 2]
        for g in range(height // ROWS):
            part = [None] * 4
            for k in range(per_block):
                rows = pl.ds(k * height + g * ROWS, ROWS)
                re = spec[rows, pl.ds(0, WIDE)]
                im = spec[rows, pl.ds(WIDE, WIDE)]
                if k > 0:
                    cos = twist[n, pl.ds(2 * k, 1), :]
                    sin = twist[n, pl.ds(2 * k + 1, 1), :]
                    re, im = re * cos - im * sin, re * sin + im * cos
                old = part[k % 4]
                part[k % 4] = (re, im) if old is None else (old[0] + re, old[1] + im)
            (r0, i0), (r1, i1), (r2, i2), (r3, i3) = part
            even_re, even_im, odd_re, odd_im = r0 + r2, i0 + i2, r1 + r3, i1 + i3
            gap_re, gap_im, far_re, far_im = r0 - r2, i0 - i2, r1 - r3, i1 - i3
            outs = (
                (even_re + odd_re, even_im + odd_im),
                (gap_re - far_im, gap_im + far_re),
                (even_re - odd_re, even_im - odd_im),
                (gap_re + far_im, gap_im - far_re),
            )
            spot = pl.ds(g * ROWS, ROWS)
            for q, pair in enumerate(outs):
                for r in range(2):
                    value = pair[r]
                    if which:
                        value = value + before[n, q, r, spot, :]
                    out[n, q, r, spot, :] = value

    done = []
    product(0)
    for n in range(count):
        if n + 1 < count:
            product(n + 1)
        combine(n)
        if not last:
            continue
        for q in range(4):
            for r in range(2):
                copy = pltpu.make_async_copy(
                    out.at[n, q, r].reshape(antennas, syms, WIDE),
                    out_ref.at[:, r, q * count + n],
                    out_sems.at[n, q, r],
                )
                copy.start()
                done.append(copy)
    for copy in done:
        copy.wait()


def transform_tables(blocks, subcarriers):
    sub = subcarriers // blocks
    tiles = blocks // WIDE
    quarter = NFFT // 4
    p = np.arange(blocks)[:, None]
    n = np.arange(quarter)[None, :]
    angle = 2.0 * np.pi / NFFT * ((sub * p - subcarriers // 2) * n % NFFT)
    cos = np.cos(angle) / math.sqrt(NFFT)
    sin = np.sin(angle) / math.sqrt(NFFT)
    count = quarter // WIDE
    table = np.stack([np.stack([cos, sin]), np.stack([-sin, cos])])
    table = table.reshape(2, 2, tiles, WIDE, count, WIDE).transpose(2, 4, 0, 3, 1, 5)
    table = table.reshape(tiles, count, 2 * WIDE, 2 * WIDE).astype(jnp.bfloat16)
    turns = 2.0 * np.pi / NFFT * (np.arange(sub)[:, None] * n)
    twist = np.stack([np.cos(turns), np.sin(turns)], 1).astype(np.float32)
    twist = twist.reshape(2 * sub, count, WIDE).transpose(1, 0, 2)
    return table, np.ascontiguousarray(twist)


def far(value):
    return pltpu.with_memory_space_constraint(value, pltpu.HBM)


def near(value):
    return pltpu.with_memory_space_constraint(value, pltpu.VMEM)


def swap(pieces):
    lanes = lax.axis_size("lane")
    return [pieces[0]] + [
        lax.ppermute(pieces[s], "lane", [(j, j ^ s) for j in range(lanes)]) for s in range(1, lanes)
    ]


def per_device(channel, symbols, layers, user_ids, user_power, neighbours, coupling):
    lanes = lax.axis_size("lane")
    cells = lax.axis_size("cell")
    _, antennas, _, order, blocks = channel.shape
    syms, subcarriers = symbols.shape[3:]
    sub = subcarriers // blocks
    chunk = blocks // lanes
    tiles = blocks // WIDE
    f32, bf16 = jnp.float32, jnp.bfloat16
    shape = jax.ShapeDtypeStruct
    table, twist = transform_tables(blocks, subcarriers)
    table, twist = jnp.asarray(table), jnp.asarray(twist)
    dma = pltpu.SemaphoreType.DMA

    amp, own, mix, turned, *pieces = pl.pallas_call(
        functools.partial(gram_kernel, lanes=lanes, chunk=chunk),
        out_shape=[pltpu.VMEM((tiles, order, WIDE), f32)]
        + [pltpu.VMEM((cells, 1, WIDE), f32)] * 2
        + [pltpu.VMEM((tiles, 2, order, antennas, WIDE), f32)]
        + [pltpu.VMEM((order * ROWS, WIDE), f32)] * lanes,
        in_specs=[HBM] * 6,
        out_specs=[VMEM] * (4 + lanes),
        scratch_shapes=[
            pltpu.VMEM((antennas, 2, order, blocks), f32),
            pltpu.VMEM((1, blocks), jnp.int32),
            pltpu.VMEM((order, blocks), jnp.int32),
            pltpu.VMEM(user_power.shape, f32),
            pltpu.SMEM(neighbours.shape, jnp.int32),
            pltpu.SMEM(coupling.shape, f32),
            pltpu.VMEM((lanes, order * ROWS, WIDE), f32),
            pltpu.VMEM((tiles, antennas * 2 * order, WIDE), f32),
            dma((5 + tiles,)),
        ],
        compiler_params=params(16),
        name="gram",
    )(*map(far, (channel, layers, user_ids, user_power, neighbours, coupling)))
    parts = swap(pieces)
    transmit = lax.all_to_all(own, "cell", 0, 0, tiled=True)

    sym, mark = pl.pallas_call(
        arrange_kernel,
        out_shape=(
            pltpu.VMEM((tiles, sub, order * 2 * syms, WIDE), f32),
            pltpu.VMEM((ROWS, WIDE), f32),
        ),
        in_specs=[HBM],
        out_specs=(VMEM, VMEM),
        scratch_shapes=[
            pltpu.VMEM(symbols.shape, bf16),
            pltpu.SemaphoreType.DMA,
            pltpu.VMEM((order * 2 * syms, subcarriers), f32),
            pltpu.VMEM((subcarriers // (sub * 32) * order * 2 * syms, sub * 32), bf16),
            pltpu.VMEM((subcarriers // (sub * 32) * order * 2 * syms, sub * 32), f32),
        ],
        compiler_params=params(16),
        cost_estimate=pl.CostEstimate(flops=10**9, bytes_accessed=8 * 10**6, transcendentals=0),
        name="arrange",
    )(far(symbols))

    packed = pl.pallas_call(
        functools.partial(solve_kernel, lanes=lanes),
        out_shape=pltpu.VMEM((order * ROWS + ROWS, WIDE), f32),
        in_specs=[VMEM] * (3 + lanes),
        out_specs=VMEM,
        scratch_shapes=[pltpu.VMEM((order * order, WIDE), f32)] * 8,
        compiler_params=params(16),
        name="solve",
    )(near(transmit), near(mix), *map(near, parts), near(mark))
    packs = swap([packed] * lanes)

    per_tile = WIDE // chunk
    height = syms * antennas
    count = NFFT // WIDE // 4
    out = ()
    for which in range(tiles):
        last = which == tiles - 1
        result = (count, 4, 2, height, WIDE)
        final = (antennas, 2, NFFT // WIDE, syms, WIDE)
        out = pl.pallas_call(
            functools.partial(transmit_kernel, which=which, last=last, chunk=chunk),
            out_shape=[shape(final, f32) if last else pltpu.VMEM(result, f32)],
            in_specs=[VMEM] * (per_tile + 3) + [HBM, VMEM] + [VMEM] * which,
            out_specs=[HBM if last else VMEM],
            scratch_shapes=[
                pltpu.VMEM((per_tile, order * ROWS + ROWS, WIDE), f32),
                pltpu.VMEM((order * order, WIDE), f32),
                pltpu.VMEM((order, WIDE), f32),
                pltpu.VMEM((2, order, antennas, WIDE), f32),
                pltpu.VMEM((2, height, WIDE), f32),
                pltpu.VMEM((sub, height, 4 * WIDE), bf16),
                pltpu.VMEM((count, 4 * WIDE, 2 * WIDE), bf16),
                pltpu.VMEM((sub * height, 2 * WIDE), f32),
                pltpu.VMEM((sub * height, 2 * WIDE), f32),
                dma((2,)),
            ]
            + [pltpu.VMEM(result, f32), dma((count, 4, 2))] * last,
            compiler_params=params(16),
            cost_estimate=pl.CostEstimate(
                flops=10**9, bytes_accessed=4 * 10**6, transcendentals=0
            ),
            name="transmit",
        )(
            *map(near, packs[which * per_tile : (which + 1) * per_tile]),
            near(amp),
            near(turned),
            near(sym),
            far(table),
            near(twist),
            *map(near, out),
        )
    out = out[0].transpose(0, 1, 3, 2, 4)
    return out.reshape(1, antennas, 2, syms, NFFT)


def solution(mesh):
    in_specs = (
        P("cell", "lane", None, None, None),
        P("cell", None, None, None, None),
        P("cell", None),
        P("cell", None, None),
        P("cell", None),
        P(),
        P(),
    )
    out_specs = P("cell", "lane", None, None, None)
    return jax.shard_map(
        per_device, mesh=mesh, in_specs=in_specs, out_specs=out_specs, check_vma=False
    )
```

time: 56.8 us -> 36.9 us (0.65)
  local copies, waits for them, and re-layouts: 14 us -> 0.01 us
  blocking collectives: 13.5 us -> 0 us
  starting transfers between devices: 8.62 us -> 13.4 us
  waiting for transfers between devices: 3.59 us -> 7.54 us
  Pallas kernels: 16.4 us -> 15.7 us
    all_to_all x1 -> x0, blocking collectives: 13.5 us -> none  [per_device(): parts = lax.all_to_all(parts, 'lane', 0, 0, tiled=True)]
    unnamed x30 -> x2, local copies, waits for them, and re-layouts: 10.9 us -> 0.01 us
    ppermute x0 -> x6, starting transfers between devices: none -> 8.06 us  [swap(): lax.ppermute(pieces[s], 'lane', [(j, j ^ s) for j in range(lanes)])]
    ppermute x0 -> x6, waiting for transfers between devices: none -> 7.54 us  [swap(): lax.ppermute(pieces[s], 'lane', [(j, j ^ s) for j in range(lanes)])]
    all_to_all x2 -> x1, waiting for transfers between devices: 3.59 us -> 0.01 us  [per_device(): transmit = lax.all_to_all(own, 'cell', 0, 0, tiled=True)]
    all_to_all x2 -> x1, starting transfers between devices: 8.62 us -> 5.31 us  [per_device(): transmit = lax.all_to_all(own, 'cell', 0, 0, tiled=True)]
    broadcast_in_dim x2 -> x0, local copies, waits for them, and re-layouts: 2.98 us -> none  [the longest x1 1.78 us: per_device(): return jnp.transpose(out, (2, 0, 1, 3))[None]]
    pallas_call x5, Pallas kernels: 16.4 us -> 15.7 us  [the longest x2 6.83 us: per_device(): pl.pallas_call(functools.partial(transmit_kernel, which=which, last=last,...]
  transfers between devices with their start and end apart: 2 -> 7, of which waited for: 2 -> 5; matrix products, arithmetic and copies ran while one was open for 0% -> 0% of each run, Pallas kernels for 6% -> 13%
where the time goes in v1:
time: 36.9 us; the launch traced here: 36.6 us
  Pallas kernels  15.7 us (43%)
  starting transfers between devices  13.4 us (36%)
  waiting for transfers between devices  7.54 us (20%)
    ppermute x6, starting transfers between devices, swap(): lax.ppermute(pieces[s], 'lane', [(j, j ^ s) for j in range(lanes)])  8.06 us
    ppermute x6, waiting for transfers between devices, swap(): lax.ppermute(pieces[s], 'lane', [(j, j ^ s) for j in range(lanes)])  7.54 us
    pallas_call x2, Pallas kernels, per_device(): pl.pallas_call(functools.partial(transmit_kernel, which=which, last=last,...  6.83 us
    all_to_all x1, starting transfers between devices, per_device(): transmit = lax.all_to_all(own, 'cell', 0, 0, tiled=True)  5.31 us
    pallas_call x1, Pallas kernels, per_device(): pl.pallas_call(functools.partial(gram_kernel, lanes=lanes, chunk=chunk),...  3.51 us
    pallas_call x1, Pallas kernels, per_device(): pl.pallas_call(functools.partial(solve_kernel, lanes=lanes), out_shape=pl...  3.17 us
    pallas_call x1, Pallas kernels, per_device(): pl.pallas_call(arrange_kernel, out_shape=(pltpu.VMEM((tiles, sub, order *...  2.14 us
  transfers between devices with their start and end apart: 7, of which 5 were waited for; matrix products, arithmetic and copies ran while one was open for 0% of the time, Pallas kernels for 13%

profile of v1, /device:TPU:0, one launch (start us, length us, event | category | flops | bytes accessed | tf_op | source)
XLA Modules:
  0.0 36.6 jit_solution(8177210590613344773)
XLA Ops:
  0.0 3.5 %gram.1 = (f32[2,16,128]{2,1,0:T(8,128)S(1)}, f32[8,1,128]{2,1,0:T(1,128)}, f32[8,1,128]{2,1,0:T(1,128)S(1)}, f32[2,2,16,16,128]{4,3,2,1,0:T(8,128)S(1)}, f32[12...) custom-call(f32[1,16,2,16,256]{4,3,2,1,0:T(8,128)} %refs_0_.1, ...), custom_call_target="tpu_custom_call" | custom-call | tf_op jit(solution)/shard_map/gram/pallas_call | solution.py:560
  3.5 0.0 copy-start
  3.5 5.3 %all-to-all-start = ((f32[8,1,128]{2,1,0:T(1,128)}), f32[8,1,128]{2,1,0:T(1,128)S(1)}, u32[]{:S(2)}, u32[]{:S(2)}) async-start(f32[8,1,128]{2,1,0:T(1,128)} %get-tuple-element.15), calls=%async_computation | async-start | bytes 8192 | tf_op jit(solution)/shard_map/all_to_all | solution.py:583
  8.8 1.6 %collective-permute-start = (f32[128,128]{1,0:T(8,128)S(1)}, f32[128,128]{1,0:T(8,128)S(1)}, u32[]{:S(2)}, u32[]{:S(2)}) collective-permute-start(f32[128,128]{1,0:T(8,128)S(1)} %get-tuple-element.18), channel_id=1, source_target_pairs={{0,1},{1,0},{2,3},{3,2},{4,5},{5,4},{6,7},{7,6},{8,9},{9,8},{10,11... | collective-permute-start | bytes 196616 | tf_op jit(solution)/shard_map/ppermute | solution.py:542
  10.4 2.6 %collective-permute-start.1 = (f32[128,128]{1,0:T(8,128)S(1)}, f32[128,128]{1,0:T(8,128)S(1)}, u32[]{:S(2)}, u32[]{:S(2)}) collective-permute-start(f32[128,128]{1,0:T(8,128)S(1)} %get-tuple-element.19), channel_id=1, source_target_pairs={{0,2},{1,3},{2,0},{3,1},{4,6},{5,7},{6,4},{7,5},{8,10},{9,11},{10,... | collective-permute-start | bytes 196616 | tf_op jit(solution)/shard_map/ppermute | solution.py:542
  13.0 0.2 collective-permute-start.2
  13.2 2.1 %arrange.1 = (f32[2,12,64,128]{3,2,1,0:T(8,128)S(1)}, f32[8,128]{1,0:T(8,128)S(1)}) custom-call(bf16[1,16,2,2,3072]{4,3,2,1,0:T(2,128)(2,1)} %far_ref.1), custom_call_target="tpu_custom_call" | custom-call | flops 1000000000 | bytes 8000000 | tf_op jit(solution)/shard_map/arrange/pallas_call | solution.py:585
  15.4 0.0 all-to-all-done.refs_0_
  15.4 0.0 collective-permute-done.refs_3_
  15.4 2.0 %collective-permute-done.1.refs_4_ = f32[128,128]{1,0:T(8,128)S(1)} collective-permute-done((f32[128,128]{1,0:T(8,128)S(1)}, f32[128,128]{1,0:T(8,128)S(1)}, u32[]{:S(2)}, u32[]{:S(2)}) %collective-permute-start.1) | collective-permute-done | bytes 65568 | tf_op jit(solution)/shard_map/ppermute | solution.py:542
  17.4 1.8 %collective-permute-done.2.refs_5_ = f32[128,128]{1,0:T(8,128)S(1)} collective-permute-done((f32[128,128]{1,0:T(8,128)S(1)}, f32[128,128]{1,0:T(8,128)S(1)}, u32[]{:S(2)}, u32[]{:S(2)}) %collective-permute-start.2) | collective-permute-done | bytes 65568 | tf_op jit(solution)/shard_map/ppermute | solution.py:542
  19.1 3.2 %solve.1.refs_0_ = f32[136,128]{1,0:T(8,128)S(1)} custom-call(f32[8,1,128]{2,1,0:T(1,128)S(1)} %all-to-all-done.refs_0_, f32[8,1,128]{2,1,0:T(1,128)S(1)} %get-tuple-element.16.refs_1_, f32[128,128]{1,0:T(8,128)S(1)} %get-tuple-element.17.refs_2_, f32[128,128]{1,0:T(8,128)S(1)} %collective-permute-done.refs_3_, ...), custom_call_target="tpu_custom_call" | custom-call | tf_op jit(solution)/shard_map/solve/pallas_call | solution.py:605
  22.3 1.2 %collective-permute-start.5 = (f32[136,128]{1,0:T(8,128)S(1)}, f32[136,128]{1,0:T(8,128)S(1)}, u32[]{:S(2)}, u32[]{:S(2)}) collective-permute-start(f32[136,128]{1,0:T(8,128)S(1)} %solve.1.refs_0_), channel_id=1, source_target_pairs={{0,1},{1,0},{2,3},{3,2},{4,5},{5,4},{6,7},{7,6},{8,9},{9,8},{10,11... | collective-permute-start | bytes 208904 | tf_op jit(solution)/shard_map/ppermute | solution.py:542
  23.5 2.4 %collective-permute-start.4 = (f32[136,128]{1,0:T(8,128)S(1)}, f32[136,128]{1,0:T(8,128)S(1)}, u32[]{:S(2)}, u32[]{:S(2)}) collective-permute-start(f32[136,128]{1,0:T(8,128)S(1)} %solve.1.refs_0_), channel_id=1, source_target_pairs={{0,3},{1,2},{2,1},{3,0},{4,7},{5,6},{6,5},{7,4},{8,11},{9,10},{10,... | collective-permute-start | bytes 208904 | tf_op jit(solution)/shard_map/ppermute | solution.py:542
  26.0 0.0 collective-permute-start.3
  26.0 0.6 %collective-permute-done.5.refs_1_ = f32[136,128]{1,0:T(8,128)S(1)} collective-permute-done((f32[136,128]{1,0:T(8,128)S(1)}, f32[136,128]{1,0:T(8,128)S(1)}, u32[]{:S(2)}, u32[]{:S(2)}) %collective-permute-start.5) | collective-permute-done | bytes 69664 | tf_op jit(solution)/shard_map/ppermute | solution.py:542
  26.6 0.0 copy-done
  26.6 2.8 %transmit.2.refs_7_ = f32[8,4,2,32,128]{4,3,2,1,0:T(8,128)S(1)} custom-call(f32[136,128]{1,0:T(8,128)S(1)} %solve.1.refs_0_, f32[136,128]{1,0:T(8,128)S(1)} %collective-permute-done.5.refs_1_, f32[2,16,128]{2,1,0:T(8,128)S(1)} %get-tuple-element.22.refs_2_, f32[2,2,16,16,128]{4,3,2,1,0:T(8,128)S(1)} %get-tuple-element.23.refs_3_, ...), custom_call_target="tpu_custom_call" | custom-call | flops 1000000000 | bytes 4000000 | tf_op jit(solution)/shard_map/transmit/pallas_call | solution.py:624
  29.4 1.0 %collective-permute-done.4.refs_1_ = f32[136,128]{1,0:T(8,128)S(1)} collective-permute-done((f32[136,128]{1,0:T(8,128)S(1)}, f32[136,128]{1,0:T(8,128)S(1)}, u32[]{:S(2)}, u32[]{:S(2)}) %collective-permute-start.4) | collective-permute-done | bytes 69664 | tf_op jit(solution)/shard_map/ppermute | solution.py:542
  30.4 2.2 %collective-permute-done.3.refs_0_ = f32[136,128]{1,0:T(8,128)S(1)} collective-permute-done((f32[136,128]{1,0:T(8,128)S(1)}, f32[136,128]{1,0:T(8,128)S(1)}, u32[]{:S(2)}, u32[]{:S(2)}) %collective-permute-start.3) | collective-permute-done | bytes 69664 | tf_op jit(solution)/shard_map/ppermute | solution.py:542
  32.6 4.1 %transmit.3 = f32[16,2,32,2,128]{4,3,2,1,0:T(2,128)} custom-call(f32[136,128]{1,0:T(8,128)S(1)} %collective-permute-done.3.refs_0_, f32[136,128]{1,0:T(8,128)S(1)} %collective-permute-done.4.refs_1_, f32[2,16,128]{2,1,0:T(8,128)S(1)} %get-tuple-element.22.refs_2_, f32[2,2,16,16,128]{4,3,2,1,0:T(8,128)S(1)} %get-tuple-element.23.refs_3_, ...), custom_call_target="tpu_custom_call" | custom-call | flops 1000000000 | bytes 4000000 | tf_op jit(solution)/shard_map/transmit/pallas_call | solution.py:624
Async XLA Ops:
  3.5 23.1 %copy-start = (f32[8,24,128]{2,1,0:T(8,128)S(1)}, f32[8,24,128]{2,1,0:T(8,128)}, u32[]{:S(2)}) copy-start(f32[8,24,128]{2,1,0:T(8,128)} %constant.5.clone.refs_6_) | copy-start | bytes 294916
  3.5 11.8 %all-to-all-start = ((f32[8,1,128]{2,1,0:T(1,128)}), f32[8,1,128]{2,1,0:T(1,128)S(1)}, u32[]{:S(2)}, u32[]{:S(2)}) async-start(f32[8,1,128]{2,1,0:T(1,128)} %get-tuple-element.15), calls=%async_computation | async-start | bytes 8192 | tf_op jit(solution)/shard_map/all_to_all | solution.py:583
  8.8 6.5 %collective-permute-start = (f32[128,128]{1,0:T(8,128)S(1)}, f32[128,128]{1,0:T(8,128)S(1)}, u32[]{:S(2)}, u32[]{:S(2)}) collective-permute-start(f32[128,128]{1,0:T(8,128)S(1)} %get-tuple-element.18), channel_id=1, source_target_pairs={{0,1},{1,0},{2,3},{3,2},{4,5},{5,4},{6,7},{7,6},{8,9},{9,8},{10,11... | collective-permute-start | bytes 196616 | tf_op jit(solution)/shard_map/ppermute | solution.py:542
  10.4 7.0 %collective-permute-start.1 = (f32[128,128]{1,0:T(8,128)S(1)}, f32[128,128]{1,0:T(8,128)S(1)}, u32[]{:S(2)}, u32[]{:S(2)}) collective-permute-start(f32[128,128]{1,0:T(8,128)S(1)} %get-tuple-element.19), channel_id=1, source_target_pairs={{0,2},{1,3},{2,0},{3,1},{4,6},{5,7},{6,4},{7,5},{8,10},{9,11},{10,... | collective-permute-start | bytes 196616 | tf_op jit(solution)/shard_map/ppermute | solution.py:542
  13.0 6.1 %collective-permute-start.2 = (f32[128,128]{1,0:T(8,128)S(1)}, f32[128,128]{1,0:T(8,128)S(1)}, u32[]{:S(2)}, u32[]{:S(2)}) collective-permute-start(f32[128,128]{1,0:T(8,128)S(1)} %get-tuple-element.20), channel_id=1, source_target_pairs={{0,3},{1,2},{2,1},{3,0},{4,7},{5,6},{6,5},{7,4},{8,11},{9,10},{10,... | collective-permute-start | bytes 196616 | tf_op jit(solution)/shard_map/ppermute | solution.py:542
  22.3 4.3 %collective-permute-start.5 = (f32[136,128]{1,0:T(8,128)S(1)}, f32[136,128]{1,0:T(8,128)S(1)}, u32[]{:S(2)}, u32[]{:S(2)}) collective-permute-start(f32[136,128]{1,0:T(8,128)S(1)} %solve.1.refs_0_), channel_id=1, source_target_pairs={{0,1},{1,0},{2,3},{3,2},{4,5},{5,4},{6,7},{7,6},{8,9},{9,8},{10,11... | collective-permute-start | bytes 208904 | tf_op jit(solution)/shard_map/ppermute | solution.py:542
  23.5 6.8 %collective-permute-start.4 = (f32[136,128]{1,0:T(8,128)S(1)}, f32[136,128]{1,0:T(8,128)S(1)}, u32[]{:S(2)}, u32[]{:S(2)}) collective-permute-start(f32[136,128]{1,0:T(8,128)S(1)} %solve.1.refs_0_), channel_id=1, source_target_pairs={{0,3},{1,2},{2,1},{3,0},{4,7},{5,6},{6,5},{7,4},{8,11},{9,10},{10,... | collective-permute-start | bytes 208904 | tf_op jit(solution)/shard_map/ppermute | solution.py:542
  26.0 6.6 %collective-permute-start.3 = (f32[136,128]{1,0:T(8,128)S(1)}, f32[136,128]{1,0:T(8,128)S(1)}, u32[]{:S(2)}, u32[]{:S(2)}) collective-permute-start(f32[136,128]{1,0:T(8,128)S(1)} %solve.1.refs_0_), channel_id=1, source_target_pairs={{0,2},{1,3},{2,0},{3,1},{4,6},{5,7},{6,4},{7,5},{8,10},{9,11},{10,... | collective-permute-start | bytes 208904 | tf_op jit(solution)/shard_map/ppermute | solution.py:542

commit v2 on v1

--- a/solution.py
+++ b/solution.py
@@ -16,6 +16,10 @@
 WIDE = 128
 HALF = WIDE // 2
 ROWS = 8
+FULL = 32760.0
+OFFSET = 32768
+ROOT_UNIT = 2.0**24
+LOG_UNIT = 2.0**23
 
 VMEM = pl.BlockSpec(memory_space=pltpu.VMEM)
 HBM = pl.BlockSpec(memory_space=pltpu.HBM)
@@ -34,6 +38,41 @@
     return value if shift == 0 else pltpu.roll(value, shift, 1)
 
 
+def mirrored(index, lanes):
+    bits = lanes.bit_length() - 1
+    total = 0
+    for b in range(bits):
+        total = total + ((index >> b) % 2) * (1 << (bits - 1 - b))
+    return total
+
+
+def split(value, unit):
+    whole = jnp.round(value * unit).astype(jnp.int32)
+    high = whole >> 16
+    return jnp.concatenate([high, whole - (high << 16) - OFFSET], 0).astype(jnp.int16)
+
+
+def joined(halves, unit):
+    high = halves[:ROWS].astype(jnp.float32) * (65536.0 / unit)
+    return high + (halves[ROWS:] + OFFSET).astype(jnp.float32) * (1.0 / unit)
+
+
+def unpacked(piece):
+    order = 2 * ROWS
+    low, rows = lane_iota() < HALF, row_iota()
+    root = joined(piece[pl.ds(order * ROWS, order), :].astype(jnp.int32), ROOT_UNIT)
+    other = pltpu.roll(root, HALF, 1)
+    both = (jnp.where(low, root, other), jnp.where(low, other, root))
+    values = {}
+    for l in range(ROWS):
+        held = piece[pl.ds(l * order, order), :].astype(jnp.int32).astype(jnp.float32)
+        for h in range(2):
+            whole = jnp.logical_and(rows == l, low if h == 0 else ~low)
+            part = jnp.where(whole, 1.0, held[h * ROWS : (h + 1) * ROWS] * (1.0 / FULL))
+            values[l, h] = root[l : l + 1] * both[h] * part
+    return values
+
+
 def params(mib):
     return pltpu.CompilerParams(vmem_limit_bytes=mib * 1024 * 1024)
 
@@ -41,7 +80,7 @@
 def gram_kernel(*refs, lanes, chunk):
     ins, outs = refs[:6], refs[10 : 10 + lanes]
     amp_all, own, mix, turned = refs[6:10]
-    channel, layers, ids_all, power, neigh, coup, pieces, stage, sems = refs[10 + lanes :]
+    channel, layers, ids_all, power, neigh, coup, pieces, inverses, stage, sems = refs[10 + lanes :]
     antennas, _, order, blocks = channel.shape
     users = power.shape[1]
     tiles = blocks // WIDE
@@ -88,7 +127,7 @@
             total = total + amp * amp
         sums.append(jnp.sum(total, axis=0, keepdims=True) / order)
     lane = lax.axis_index("lane")
-    start = lane * chunk
+    start = mirrored(lane, lanes) * chunk
     mine = jnp.broadcast_to(sums[0], (ROWS, WIDE))
     for t in range(1, tiles):
         mine = jnp.where(start // WIDE == t, jnp.broadcast_to(sums[t], (ROWS, WIDE)), mine)
@@ -107,6 +146,27 @@
         granted = layers[:, spot]
         inside = [rows + h * ROWS < granted for h in range(2)]
         large[t].wait()
+        inverse, root = [], []
+        for h in range(2):
+            part = pl.ds(h * ROWS, ROWS)
+            total = jnp.zeros((ROWS, WIDE), jnp.float32)
+            for a in range(antennas):
+                re, im = channel[a, 0, part, spot], channel[a, 1, part, spot]
+                total = total + (re * re + im * im)
+            total = jnp.where(inside[h], total, 0.0)
+            inverse.append(jnp.where(total > 0.0, lax.rsqrt(total), 0.0))
+            root.append(total * inverse[h])
+            inverses[part, :] = inverse[h] * FULL
+        chunks = range(t * WIDE // chunk, (t + 1) * WIDE // chunk)
+
+        def packed(top, bottom, z):
+            off = z * chunk - t * WIDE
+            return jnp.where(low, turn(top, -off), turn(bottom, HALF - off))
+
+        for z in chunks:
+            pieces[lane ^ mirrored(z, lanes), pl.ds(order * ROWS, order), :] = split(
+                packed(root[0], root[1], z), ROOT_UNIT
+            )
         for base in range(0, ROWS, 2):
             tops = (base, base + 1)
             acc = {}
@@ -141,15 +201,19 @@
                     acc[g, "im", 0],
                     jnp.where(rows >= l, acc[g, "re", 1], acc[g, "im", 1]),
                 ]
+                tops_out, bottoms_out = [], []
                 for h in range(2):
                     top = jnp.where(jnp.logical_and(inside[h], here), upper[h], 0.0)
                     bottom = jnp.where(jnp.logical_and(inside[h], there), lower[h], 0.0)
-                    for z in range(t * WIDE // chunk, (t + 1) * WIDE // chunk):
-                        off = z * chunk - t * WIDE
-                        where = pl.ds(l * 2 * ROWS + h * ROWS, ROWS)
-                        pieces[lane ^ z, where, :] = jnp.where(
-                            low, turn(top, -off), turn(bottom, HALF - off)
-                        )
+                    tops_out.append(top * inverses[pl.ds(l, 1), :] * inverse[h])
+                    bottoms_out.append(bottom * inverses[pl.ds(g, 1), :] * inverse[h])
+                for z in chunks:
+                    value = jnp.concatenate(
+                        [packed(tops_out[h], bottoms_out[h], z) for h in range(2)], 0
+                    )
+                    pieces[lane ^ mirrored(z, lanes), pl.ds(l * order, order), :] = (
+                        jnp.round(value).astype(jnp.int32).astype(jnp.int16)
+                    )
     for s in range(lanes):
         outs[s][...] = pieces[s]
     for t in range(tiles):
@@ -168,10 +232,10 @@
                     ]
 
 
-def solve_kernel(*refs, lanes):
+def solve_kernel(*refs, count):
     trans, mix = refs[:2]
-    parts, out = refs[2 : 2 + lanes], refs[3 + lanes]
-    pack, gram, e_a, e_b, s_a, s_b, d_re, d_im = refs[4 + lanes :]
+    parts, out = refs[2 : 2 + count], refs[2 + count]
+    pack, gram, e_a, e_b, s_a, s_b, d_re, d_im = refs[3 + count :]
     order = 2 * ROWS
     low = lane_iota() < HALF
     rows = row_iota()
@@ -186,11 +250,12 @@
     def row(ref, l, k):
         return ref[pl.ds(l * order + k, 1), :]
 
+    others = [unpacked(part) for part in parts[1:]]
     for l in range(ROWS):
         for h in range(2):
             value = parts[0][at(l, h), :]
-            for s in range(1, lanes):
-                value = value + parts[s][at(l, h), :]
+            for other in others:
+                value = value + other[l, h]
             other = pltpu.roll(value, HALF, 1)
             pack[at(l, h), :] = jnp.where(low, value, other)
             pack[at(l + ROWS, h), :] = jnp.where(low, other, value)
@@ -286,28 +351,56 @@
     spread(s_a)
     products([(gram, e_a, None)])
 
-    energy = []
+    logs, norms = [], []
     for h in range(2):
         value = s_a[at(0, h), :] * e_a[at(0, h), :]
         for m in range(1, order):
             value = value + s_a[at(m, h), :] * e_a[at(m, h), :]
-        energy.append(value + pltpu.roll(value, HALF, 1))
-    last = jnp.where(low, energy[0], energy[1])
+        energy = value + pltpu.roll(value, HALF, 1)
+        norms.append(lax.rsqrt(jnp.maximum(energy, 0.0) + NORM_EPS))
+        logs.append(jnp.log2(norms[h]))
+        d_re[pl.ds(h * ROWS, ROWS), :] = norms[h]
+    peak = jnp.zeros((ROWS, WIDE), jnp.float32)
+    diagonal = [peak, peak]
+    for l in range(order):
+        for h in range(2) if l < ROWS else (1,):
+            value = s_a[at(l, h), :] * d_re[pl.ds(l, 1), :] * norms[h]
+            if h * ROWS <= l < h * ROWS + ROWS:
+                spot = rows + h * ROWS == l
+                diagonal[h] = jnp.where(spot, value, diagonal[h])
+                value = jnp.where(spot, 0.0, value)
+            peak = jnp.maximum(peak, jnp.abs(value))
+    peak = jnp.max(peak, axis=0, keepdims=True)
+    peak = jnp.maximum(jnp.broadcast_to(peak, (ROWS, WIDE)), 1e-18)
+    level = jnp.ceil(jnp.log2(jnp.maximum(peak, pltpu.roll(peak, HALF, 1))) * 128.0) + 1.0
+    shrink = jnp.exp2(level * (-1.0 / 128.0))
+    norms = [norm * shrink for norm in norms]
     for l in range(ROWS):
+        values = []
         for h in range(2):
             first = s_a[at(l, h), :]
             second = s_a[at(l + ROWS, h), :]
             where = rows + h * ROWS
+            first = jnp.where(where >= l, first, pltpu.roll(first, HALF, 1))
+            second = jnp.where(where >= l + ROWS, pltpu.roll(second, HALF, 1), second)
             value = jnp.where(
-                low,
-                jnp.where(where >= l, first, pltpu.roll(first, HALF, 1)),
-                jnp.where(where >= l + ROWS, pltpu.roll(second, HALF, 1), second),
+                low, first * d_re[pl.ds(l, 1), :], second * d_re[pl.ds(l + ROWS, 1), :]
             )
-            out[at(l, h), :] = value
-    out[pl.ds(order * ROWS, ROWS), :] = last
-
-
-def arrange_kernel(far_ref, sym_ref, mark_ref, symbols_ref, sem, flat, stacked, moved):
+            value = jnp.round(value * norms[h] * FULL)
+            here = jnp.logical_and(rows == l, low if h == 0 else ~low)
+            values.append(jnp.where(here, level, value))
+        out[pl.ds(l * order, order), :] = (
+            jnp.concatenate(values, 0).astype(jnp.int32).astype(jnp.int16)
+        )
+    diagonal = [jnp.where(low, d, pltpu.roll(d, HALF, 1)) for d in diagonal]
+    diagonal = [jnp.log2(jnp.maximum(d * shrink, 1e-30)) for d in diagonal]
+    out[pl.ds(order * ROWS, order), :] = split(jnp.where(low, *diagonal), LOG_UNIT)
+    out[pl.ds(order * ROWS + order, order), :] = split(jnp.where(low, *logs), LOG_UNIT)
+
+
+def arrange_kernel(
+    far_ref, own_ref, other_ref, sym_ref, sum_ref, symbols_ref, sem, flat, stacked, moved
+):
     copy = pltpu.make_async_copy(far_ref, symbols_ref, sem)
     copy.start()
     copy.wait()
@@ -336,25 +429,27 @@
                     piece = turn(piece, (b - k % quads) * few)
                     value = piece if b == 0 else jnp.where(lanes >= b * few, piece, value)
                 sym_ref[t, k, pl.ds(g * ROWS, ROWS), :] = value
-    mark_ref[...] = jnp.zeros(mark_ref.shape, jnp.float32)
-
-
-def transmit_kernel(*refs, which, last, chunk):
+    own, other = unpacked(own_ref), unpacked(other_ref)
+    for (l, h), value in own.items():
+        sum_ref[pl.ds((l * 2 + h) * ROWS, ROWS), :] = value + other[l, h]
+
+
+def transmit_kernel(*refs, which, last, lanes_count, chunk):
     per_tile = WIDE // chunk
     ins, rest = refs[:per_tile], refs[per_tile:]
     amp, chan, sym, table_ref, twist = rest[:5]
     before = rest[5] if which else None
     out_ref = out = rest[5 + which]
-    packs, pack, scale, weight, mixed, grid, table, spec_a, spec_b, sems = rest[
-        6 + which : 16 + which
+    packs, pack, whole, norm, scale, scaled, weight, mixed, grid, table, spec_a, spec_b, sems = rest[
+        6 + which : 19 + which
     ]
     if last:
-        out, out_sems = rest[16 + which :]
+        out, out_sems = rest[19 + which :]
     tiles, _, order, antennas, _ = chan.shape
     per_block, syms = sym.shape[1], sym.shape[2] // (2 * order)
     groups = antennas // ROWS
     lanes = lane_iota()
-    lane = lax.axis_index("lane")
+    lane = mirrored(lax.axis_index("lane"), lanes_count)
     tile = (lane // per_tile) ^ which
     halves = [
         pltpu.make_async_copy(
@@ -367,22 +462,46 @@
 
     for s, ref in enumerate(ins):
         packs[lane % per_tile ^ s] = ref[...]
-    for i in range(2 * ROWS + 1):
-        rows = pl.ds(i * ROWS, ROWS)
-        value = packs[0, rows, :]
-        first, second = value, pltpu.roll(value, HALF, 1)
+
+    def merged(values):
+        first, second = values[0], pltpu.roll(values[0], HALF, 1)
         for z in range(1, per_tile):
             off = z * chunk
-            value = packs[z, rows, :]
-            first = jnp.where(lanes >= off, turn(value, off), first)
-            second = jnp.where(lanes >= off, turn(value, off - HALF), second)
-        if i < 2 * ROWS:
-            pack[rows, :] = first
-            pack[pl.ds((i + 2 * ROWS) * ROWS, ROWS), :] = second
-        else:
-            for h, energy in enumerate((first, second)):
-                spot = pl.ds(h * ROWS, ROWS)
-                scale[spot, :] = amp[tile, spot, :] / jnp.sqrt(energy + NORM_EPS)
+            first = jnp.where(lanes >= off, turn(values[z], off), first)
+            second = jnp.where(lanes >= off, turn(values[z], off - HALF), second)
+        return first, second
+
+    for l in range(ROWS):
+        held = [
+            packs[z, pl.ds(l * order, order), :].astype(jnp.int32).astype(jnp.float32)
+            for z in range(per_tile)
+        ]
+        for h in range(2):
+            both = merged([value[h * ROWS : (h + 1) * ROWS] for value in held])
+            for i, value in enumerate(both):
+                pack[pl.ds((l + i * ROWS) * order + h * ROWS, ROWS), :] = value
+    grow = jnp.exp2(pack[pl.ds(0, 1), :] * (1.0 / 128.0)) * (1.0 / FULL)
+    tails = [
+        merged(
+            [
+                joined(
+                    packs[z, pl.ds(order * ROWS + i * order, order), :].astype(jnp.int32), LOG_UNIT
+                )
+                for z in range(per_tile)
+            ]
+        )
+        for i in range(2)
+    ]
+    for h in range(2):
+        spot = pl.ds(h * ROWS, ROWS)
+        whole[spot, :] = jnp.exp2(tails[0][h]) * FULL
+        norm[spot, :] = jnp.exp2(-tails[1][h])
+        scale[spot, :] = amp[tile, spot, :] * grow
+    for r in range(2):
+        for m in range(order):
+            for g in range(groups):
+                spot = pl.ds(g * ROWS, ROWS)
+                scaled[r, m, spot, :] = chan[tile, r, m, spot, :] * norm[pl.ds(m, 1), :]
 
     def row(l, m):
         return pack[pl.ds(l * order + m, 1), :]
@@ -395,11 +514,10 @@
 
         for m in range(order):
             here = [
-                [chan[tile, r, m, pl.ds(g * ROWS, ROWS), :] for g in range(groups)]
-                for r in range(2)
+                [scaled[r, m, pl.ds(g * ROWS, ROWS), :] for g in range(groups)] for r in range(2)
             ]
             for l in range(base, base + 4):
-                inv_re = row(min(l, m), max(l, m))
+                inv_re = row(min(l, m), max(l, m)) if l != m else whole[pl.ds(l, 1), :]
                 inv_im = row(max(l, m), min(l, m)) if l != m else None
                 if l > m:
                     inv_im = -inv_im
@@ -437,10 +555,10 @@
                     spot = pl.ds(g * ROWS * syms + s, ROWS, stride=syms)
                     mixed[r, spot, :] = acc[s, g][r]
         for r in range(2):
-            whole = mixed[r]
-            high = whole.astype(jnp.bfloat16)
+            exact = mixed[r]
+            high = exact.astype(jnp.bfloat16)
             grid[k, :, pl.ds(r * WIDE, WIDE)] = high
-            grid[k, :, pl.ds((2 + r) * WIDE, WIDE)] = (whole - high.astype(jnp.float32)).astype(
+            grid[k, :, pl.ds((2 + r) * WIDE, WIDE)] = (exact - high.astype(jnp.float32)).astype(
                 jnp.bfloat16
             )
         return carry
@@ -562,7 +680,7 @@
         out_shape=[pltpu.VMEM((tiles, order, WIDE), f32)]
         + [pltpu.VMEM((cells, 1, WIDE), f32)] * 2
         + [pltpu.VMEM((tiles, 2, order, antennas, WIDE), f32)]
-        + [pltpu.VMEM((order * ROWS, WIDE), f32)] * lanes,
+        + [pltpu.VMEM((order * ROWS + order, WIDE), jnp.int16)] * lanes,
         in_specs=[HBM] * 6,
         out_specs=[VMEM] * (4 + lanes),
         scratch_shapes=[
@@ -572,7 +690,8 @@
             pltpu.VMEM(user_power.shape, f32),
             pltpu.SMEM(neighbours.shape, jnp.int32),
             pltpu.SMEM(coupling.shape, f32),
-            pltpu.VMEM((lanes, order * ROWS, WIDE), f32),
+            pltpu.VMEM((lanes, order * ROWS + order, WIDE), jnp.int16),
+            pltpu.VMEM((order, WIDE), f32),
             pltpu.VMEM((tiles, antennas * 2 * order, WIDE), f32),
             dma((5 + tiles,)),
         ],
@@ -582,13 +701,13 @@
     parts = swap(pieces)
     transmit = lax.all_to_all(own, "cell", 0, 0, tiled=True)
 
-    sym, mark = pl.pallas_call(
+    sym, pair = pl.pallas_call(
         arrange_kernel,
         out_shape=(
             pltpu.VMEM((tiles, sub, order * 2 * syms, WIDE), f32),
-            pltpu.VMEM((ROWS, WIDE), f32),
+            pltpu.VMEM((order * ROWS, WIDE), f32),
         ),
-        in_specs=[HBM],
+        in_specs=[HBM, VMEM, VMEM],
         out_specs=(VMEM, VMEM),
         scratch_shapes=[
             pltpu.VMEM(symbols.shape, bf16),
@@ -600,18 +719,20 @@
         compiler_params=params(16),
         cost_estimate=pl.CostEstimate(flops=10**9, bytes_accessed=8 * 10**6, transcendentals=0),
         name="arrange",
-    )(far(symbols))
+    )(far(symbols), near(parts[0]), near(parts[lanes // 2]))
+    parts = [pair] + [part for s, part in enumerate(parts) if s not in (0, lanes // 2)]
 
     packed = pl.pallas_call(
-        functools.partial(solve_kernel, lanes=lanes),
-        out_shape=pltpu.VMEM((order * ROWS + ROWS, WIDE), f32),
-        in_specs=[VMEM] * (3 + lanes),
+        functools.partial(solve_kernel, count=lanes - 1),
+        out_shape=pltpu.VMEM((order * ROWS + 2 * order, WIDE), jnp.int16),
+        in_specs=[VMEM] * (1 + lanes),
         out_specs=VMEM,
         scratch_shapes=[pltpu.VMEM((order * order, WIDE), f32)] * 8,
         compiler_params=params(16),
         name="solve",
-    )(near(transmit), near(mix), *map(near, parts), near(mark))
+    )(near(transmit), near(mix), *map(near, parts))
     packs = swap([packed] * lanes)
+    packs = [packs[mirrored(i, lanes)] for i in range(lanes)]
 
     per_tile = WIDE // chunk
     height = syms * antennas
@@ -622,14 +743,19 @@
         result = (count, 4, 2, height, WIDE)
         final = (antennas, 2, NFFT // WIDE, syms, WIDE)
         out = pl.pallas_call(
-            functools.partial(transmit_kernel, which=which, last=last, chunk=chunk),
+            functools.partial(
+                transmit_kernel, which=which, last=last, lanes_count=lanes, chunk=chunk
+            ),
             out_shape=[shape(final, f32) if last else pltpu.VMEM(result, f32)],
             in_specs=[VMEM] * (per_tile + 3) + [HBM, VMEM] + [VMEM] * which,
             out_specs=[HBM if last else VMEM],
             scratch_shapes=[
-                pltpu.VMEM((per_tile, order * ROWS + ROWS, WIDE), f32),
+                pltpu.VMEM((per_tile, order * ROWS + 2 * order, WIDE), jnp.int16),
                 pltpu.VMEM((order * order, WIDE), f32),
                 pltpu.VMEM((order, WIDE), f32),
+                pltpu.VMEM((order, WIDE), f32),
+                pltpu.VMEM((order, WIDE), f32),
+                pltpu.VMEM((2, order, antennas, WIDE), f32),
                 pltpu.VMEM((2, order, antennas, WIDE), f32),
                 pltpu.VMEM((2, height, WIDE), f32),
                 pltpu.VMEM((sub, height, 4 * WIDE), bf16),

time: 36.9 us -> 33.8 us (0.916)
  waiting for transfers between devices: 7.54 us -> 4.8 us
    ppermute x6, waiting for transfers between devices: 7.54 us -> 4.17 us  [swap(): lax.ppermute(pieces[s], 'lane', [(j, j ^ s) for j in range(lanes)])]
    all_to_all x1, starting transfers between devices: 5.31 us -> 3.72 us  [per_device(): transmit = lax.all_to_all(own, 'cell', 0, 0, tiled=True)]
    ppermute x6, starting transfers between devices: 8.06 us -> 9.45 us  [swap(): lax.ppermute(pieces[s], 'lane', [(j, j ^ s) for j in range(lanes)])]
    all_to_all x1, waiting for transfers between devices: 0.01 us -> 0.63 us  [per_device(): transmit = lax.all_to_all(own, 'cell', 0, 0, tiled=True)]
    pallas_call x1, Pallas kernels: 3.51 us -> 3.1 us  [per_device(): pl.pallas_call(functools.partial(gram_kernel, lanes=lanes, chunk=chunk),...]
  transfers between devices with their start and end apart: 7 -> 7, of which waited for: 5 -> 3; matrix products, arithmetic and copies ran while one was open for 0% -> 0% of each run, Pallas kernels for 13% -> 15%
where the time goes in v2:
time: 33.8 us; the launch traced here: 33.5 us
  Pallas kernels  15.5 us (46%)
  starting transfers between devices  13.2 us (39%)
  waiting for transfers between devices  4.8 us (14%)
    ppermute x6, starting transfers between devices, swap(): lax.ppermute(pieces[s], 'lane', [(j, j ^ s) for j in range(lanes)])  9.45 us
    pallas_call x2, Pallas kernels, per_device(): pl.pallas_call(functools.partial(transmit_kernel, which=which, last=last,...  6.85 us
    ppermute x6, waiting for transfers between devices, swap(): lax.ppermute(pieces[s], 'lane', [(j, j ^ s) for j in range(lanes)])  4.17 us
    all_to_all x1, starting transfers between devices, per_device(): transmit = lax.all_to_all(own, 'cell', 0, 0, tiled=True)  3.72 us
    pallas_call x1, Pallas kernels, per_device(): pl.pallas_call(functools.partial(solve_kernel, count=lanes - 1), out_shap...  3.4 us
    pallas_call x1, Pallas kernels, per_device(): pl.pallas_call(functools.partial(gram_kernel, lanes=lanes, chunk=chunk),...  3.1 us
    pallas_call x1, Pallas kernels, per_device(): pl.pallas_call(arrange_kernel, out_shape=(pltpu.VMEM((tiles, sub, order *...  2.14 us
  transfers between devices with their start and end apart: 7, of which 3 were waited for; matrix products, arithmetic and copies ran while one was open for 0% of the time, Pallas kernels for 15%

profile of v2, /device:TPU:0, one launch (start us, length us, event | category | flops | bytes accessed | tf_op | source)
XLA Modules:
  0.0 33.5 jit_solution(12261660778494678101)
XLA Ops:
  0.0 0.0 copy-start
  0.0 3.1 %gram.1 = (f32[2,16,128]{2,1,0:T(8,128)S(1)}, f32[8,1,128]{2,1,0:T(1,128)}, f32[8,1,128]{2,1,0:T(1,128)S(1)}, f32[2,2,16,16,128]{4,3,2,1,0:T(8,128)S(1)}, s16[14...) custom-call(f32[1,16,2,16,256]{4,3,2,1,0:T(8,128)} %refs_0_.1, ...), custom_call_target="tpu_custom_call" | custom-call | tf_op jit(solution)/shard_map/gram/pallas_call | solution.py:678
  3.1 4.1 %collective-permute-start = (s16[144,128]{1,0:T(8,128)(2,1)S(1)}, s16[144,128]{1,0:T(8,128)(2,1)S(1)}, u32[]{:S(2)}, u32[]{:S(2)}) collective-permute-start(s16[144,128]{1,0:T(8,128)(2,1)S(1)} %get-tuple-element.18), channel_id=1, source_target_pairs={{0,2},{1,3},{2,0},{3,1},{4,6},{5,7},{6,4},{7,5},{8,10},{9,11},{10,... | collective-permute-start | bytes 110600 | tf_op jit(solution)/shard_map/ppermute | solution.py:660
  7.2 3.7 %all-to-all-start = ((f32[8,1,128]{2,1,0:T(1,128)}), f32[8,1,128]{2,1,0:T(1,128)S(1)}, u32[]{:S(2)}, u32[]{:S(2)}) async-start(f32[8,1,128]{2,1,0:T(1,128)} %get-tuple-element.15), calls=%async_computation | async-start | bytes 8192 | tf_op jit(solution)/shard_map/all_to_all | solution.py:702
  10.9 1.6 %collective-permute-start.1 = (s16[144,128]{1,0:T(8,128)(2,1)S(1)}, s16[144,128]{1,0:T(8,128)(2,1)S(1)}, u32[]{:S(2)}, u32[]{:S(2)}) collective-permute-start(s16[144,128]{1,0:T(8,128)(2,1)S(1)} %get-tuple-element.20), channel_id=1, source_target_pairs={{0,1},{1,0},{2,3},{3,2},{4,5},{5,4},{6,7},{7,6},{8,9},{9,8},{10,11... | collective-permute-start | bytes 110600 | tf_op jit(solution)/shard_map/ppermute | solution.py:660
  12.5 0.2 collective-permute-start.2
  12.7 0.0 collective-permute-done.other_ref
  12.7 2.1 %arrange.1 = (f32[2,12,64,128]{3,2,1,0:T(8,128)S(1)}, f32[128,128]{1,0:T(8,128)S(1)}) custom-call(bf16[1,16,2,2,3072]{4,3,2,1,0:T(2,128)(2,1)} %far_ref.1, s16[144,128]{1,0:T(8,128)(2,1)S(1)} %get-tuple-element.17.own_ref, s16[144,128]{1,0:T(8,128)(2,1)S(1)} %collective-permute-done.other_ref), custom_call_target="tpu_custom_call" | custom-call | flops 1000000000 | bytes 8000000 | tf_op jit(solution)/shard_map/arrange/pallas_call | solution.py:704
  14.9 0.6 %all-to-all-done.refs_0_ = f32[8,1,128]{2,1,0:T(1,128)S(1)} async-done(((f32[8,1,128]{2,1,0:T(1,128)}), f32[8,1,128]{2,1,0:T(1,128)S(1)}, u32[]{:S(2)}, u32[]{:S(2)}) %all-to-all-start) | async-done | bytes 4128 | tf_op jit(solution)/shard_map/all_to_all | solution.py:702
  15.5 0.0 collective-permute-done.1.refs_3_
  15.5 2.7 %collective-permute-done.2.refs_4_ = s16[144,128]{1,0:T(8,128)(2,1)S(1)} collective-permute-done((s16[144,128]{1,0:T(8,128)(2,1)S(1)}, s16[144,128]{1,0:T(8,128)(2,1)S(1)}, u32[]{:S(2)}, u32[]{:S(2)}) %collective-permute-start.2) | collective-permute-done | bytes 36896 | tf_op jit(solution)/shard_map/ppermute | solution.py:660
  18.3 3.4 %solve.1.refs_0_ = s16[160,128]{1,0:T(8,128)(2,1)S(1)} custom-call(f32[8,1,128]{2,1,0:T(1,128)S(1)} %all-to-all-done.refs_0_, f32[8,1,128]{2,1,0:T(1,128)S(1)} %get-tuple-element.16.refs_1_, f32[128,128]{1,0:T(8,128)S(1)} %get-tuple-element.19.refs_2_, s16[144,128]{1,0:T(8,128)(2,1)S(1)} %collective-permute-done.1.refs_3_, ...), custom_call_target="tpu_custom_call" | custom-call | tf_op jit(solution)/shard_map/solve/pallas_call | solution.py:725
  21.7 0.1 collective-permute-start.5
  21.8 1.2 %collective-permute-start.4 = (s16[160,128]{1,0:T(8,128)(2,1)S(1)}, s16[160,128]{1,0:T(8,128)(2,1)S(1)}, u32[]{:S(2)}, u32[]{:S(2)}) collective-permute-start(s16[160,128]{1,0:T(8,128)(2,1)S(1)} %solve.1.refs_0_), channel_id=1, source_target_pairs={{0,3},{1,2},{2,1},{3,0},{4,7},{5,6},{6,5},{7,4},{8,11},{9,10},{10,... | collective-permute-start | bytes 122888 | tf_op jit(solution)/shard_map/ppermute | solution.py:660
  22.9 2.3 %collective-permute-start.3 = (s16[160,128]{1,0:T(8,128)(2,1)S(1)}, s16[160,128]{1,0:T(8,128)(2,1)S(1)}, u32[]{:S(2)}, u32[]{:S(2)}) collective-permute-start(s16[160,128]{1,0:T(8,128)(2,1)S(1)} %solve.1.refs_0_), channel_id=1, source_target_pairs={{0,1},{1,0},{2,3},{3,2},{4,5},{5,4},{6,7},{7,6},{8,9},{9,8},{10,11... | collective-permute-start | bytes 122888 | tf_op jit(solution)/shard_map/ppermute | solution.py:660
  25.2 1.4 %collective-permute-done.5.refs_1_ = s16[160,128]{1,0:T(8,128)(2,1)S(1)} collective-permute-done((s16[160,128]{1,0:T(8,128)(2,1)S(1)}, s16[160,128]{1,0:T(8,128)(2,1)S(1)}, u32[]{:S(2)}, u32[]{:S(2)}) %collective-permute-start.5) | collective-permute-done | bytes 40992 | tf_op jit(solution)/shard_map/ppermute | solution.py:660
  26.6 0.0 copy-done
  26.6 2.8 %transmit.2.refs_7_ = f32[8,4,2,32,128]{4,3,2,1,0:T(8,128)S(1)} custom-call(s16[160,128]{1,0:T(8,128)(2,1)S(1)} %solve.1.refs_0_, s16[160,128]{1,0:T(8,128)(2,1)S(1)} %collective-permute-done.5.refs_1_, f32[2,16,128]{2,1,0:T(8,128)S(1)} %get-tuple-element.22.refs_2_, f32[2,2,16,16,128]{4,3,2,1,0:T(8,128)S(1)} %get-tuple-element.23.refs_3_, ...), custom_call_target="tpu_custom_call" | custom-call | flops 1000000000 | bytes 4000000 | tf_op jit(solution)/shard_map/transmit/pallas_call | solution.py:745
  29.4 0.0 collective-permute-done.4.refs_1_
  29.5 0.0 collective-permute-done.3.refs_0_
  29.5 4.1 %transmit.3 = f32[16,2,32,2,128]{4,3,2,1,0:T(2,128)} custom-call(s16[160,128]{1,0:T(8,128)(2,1)S(1)} %collective-permute-done.3.refs_0_, s16[160,128]{1,0:T(8,128)(2,1)S(1)} %collective-permute-done.4.refs_1_, f32[2,16,128]{2,1,0:T(8,128)S(1)} %get-tuple-element.22.refs_2_, f32[2,2,16,16,128]{4,3,2,1,0:T(8,128)S(1)} %get-tuple-element.23.refs_3_, ...), custom_call_target="tpu_custom_call" | custom-call | flops 1000000000 | bytes 4000000 | tf_op jit(solution)/shard_map/transmit/pallas_call | solution.py:745
Async XLA Ops:
  0.0 26.6 %copy-start = (f32[8,24,128]{2,1,0:T(8,128)S(1)}, f32[8,24,128]{2,1,0:T(8,128)}, u32[]{:S(2)}) copy-start(f32[8,24,128]{2,1,0:T(8,128)} %constant.5.clone.refs_6_) | copy-start | bytes 294916
  3.1 9.6 %collective-permute-start = (s16[144,128]{1,0:T(8,128)(2,1)S(1)}, s16[144,128]{1,0:T(8,128)(2,1)S(1)}, u32[]{:S(2)}, u32[]{:S(2)}) collective-permute-start(s16[144,128]{1,0:T(8,128)(2,1)S(1)} %get-tuple-element.18), channel_id=1, source_target_pairs={{0,2},{1,3},{2,0},{3,1},{4,6},{5,7},{6,4},{7,5},{8,10},{9,11},{10,... | collective-permute-start | bytes 110600 | tf_op jit(solution)/shard_map/ppermute | solution.py:660
  7.2 8.3 %all-to-all-start = ((f32[8,1,128]{2,1,0:T(1,128)}), f32[8,1,128]{2,1,0:T(1,128)S(1)}, u32[]{:S(2)}, u32[]{:S(2)}) async-start(f32[8,1,128]{2,1,0:T(1,128)} %get-tuple-element.15), calls=%async_computation | async-start | bytes 8192 | tf_op jit(solution)/shard_map/all_to_all | solution.py:702
  10.9 4.6 %collective-permute-start.1 = (s16[144,128]{1,0:T(8,128)(2,1)S(1)}, s16[144,128]{1,0:T(8,128)(2,1)S(1)}, u32[]{:S(2)}, u32[]{:S(2)}) collective-permute-start(s16[144,128]{1,0:T(8,128)(2,1)S(1)} %get-tuple-element.20), channel_id=1, source_target_pairs={{0,1},{1,0},{2,3},{3,2},{4,5},{5,4},{6,7},{7,6},{8,9},{9,8},{10,11... | collective-permute-start | bytes 110600 | tf_op jit(solution)/shard_map/ppermute | solution.py:660
  12.5 5.8 %collective-permute-start.2 = (s16[144,128]{1,0:T(8,128)(2,1)S(1)}, s16[144,128]{1,0:T(8,128)(2,1)S(1)}, u32[]{:S(2)}, u32[]{:S(2)}) collective-permute-start(s16[144,128]{1,0:T(8,128)(2,1)S(1)} %get-tuple-element.21), channel_id=1, source_target_pairs={{0,3},{1,2},{2,1},{3,0},{4,7},{5,6},{6,5},{7,4},{8,11},{9,10},{10,... | collective-permute-start | bytes 110600 | tf_op jit(solution)/shard_map/ppermute | solution.py:660
  21.7 5.0 %collective-permute-start.5 = (s16[160,128]{1,0:T(8,128)(2,1)S(1)}, s16[160,128]{1,0:T(8,128)(2,1)S(1)}, u32[]{:S(2)}, u32[]{:S(2)}) collective-permute-start(s16[160,128]{1,0:T(8,128)(2,1)S(1)} %solve.1.refs_0_), channel_id=1, source_target_pairs={{0,2},{1,3},{2,0},{3,1},{4,6},{5,7},{6,4},{7,5},{8,10},{9,11},{10,... | collective-permute-start | bytes 122888 | tf_op jit(solution)/shard_map/ppermute | solution.py:660
  21.8 7.7 %collective-permute-start.4 = (s16[160,128]{1,0:T(8,128)(2,1)S(1)}, s16[160,128]{1,0:T(8,128)(2,1)S(1)}, u32[]{:S(2)}, u32[]{:S(2)}) collective-permute-start(s16[160,128]{1,0:T(8,128)(2,1)S(1)} %solve.1.refs_0_), channel_id=1, source_target_pairs={{0,3},{1,2},{2,1},{3,0},{4,7},{5,6},{6,5},{7,4},{8,11},{9,10},{10,... | collective-permute-start | bytes 122888 | tf_op jit(solution)/shard_map/ppermute | solution.py:660
  22.9 6.5 %collective-permute-start.3 = (s16[160,128]{1,0:T(8,128)(2,1)S(1)}, s16[160,128]{1,0:T(8,128)(2,1)S(1)}, u32[]{:S(2)}, u32[]{:S(2)}) collective-permute-start(s16[160,128]{1,0:T(8,128)(2,1)S(1)} %solve.1.refs_0_), channel_id=1, source_target_pairs={{0,1},{1,0},{2,3},{3,2},{4,5},{5,4},{6,7},{7,6},{8,9},{9,8},{10,11... | collective-permute-start | bytes 122888 | tf_op jit(solution)/shard_map/ppermute | solution.py:660

commit v3 on v2

--- a/solution.py
+++ b/solution.py
@@ -78,9 +78,9 @@
 
 
 def gram_kernel(*refs, lanes, chunk):
-    ins, outs = refs[:6], refs[10 : 10 + lanes]
-    amp_all, own, mix, turned = refs[6:10]
-    channel, layers, ids_all, power, neigh, coup, pieces, inverses, stage, sems = refs[10 + lanes :]
+    ins, outs = refs[:6], refs[9 : 9 + lanes]
+    amp_all, own, mix = refs[6:9]
+    channel, layers, ids_all, power, neigh, coup, pieces, inverses, sems = refs[9 + lanes :]
     antennas, _, order, blocks = channel.shape
     users = power.shape[1]
     tiles = blocks // WIDE
@@ -216,20 +216,6 @@
                     )
     for s in range(lanes):
         outs[s][...] = pieces[s]
-    for t in range(tiles):
-        for a in range(antennas):
-            for r in range(2):
-                for h in range(order // ROWS):
-                    stage[t, pl.ds((a * 2 + r) * order + h * ROWS, ROWS), :] = channel[
-                        a, r, pl.ds(h * ROWS, ROWS), pl.ds(t * WIDE, WIDE)
-                    ]
-        for r in range(2):
-            for m in range(order):
-                for h in range(antennas // ROWS):
-                    first = h * ROWS * 2 * order + r * order + m
-                    turned[t, r, m, pl.ds(h * ROWS, ROWS), :] = stage[
-                        t, pl.ds(first, ROWS, stride=2 * order), :
-                    ]
 
 
 def solve_kernel(*refs, count):
@@ -399,11 +385,29 @@
 
 
 def arrange_kernel(
-    far_ref, own_ref, other_ref, sym_ref, sum_ref, symbols_ref, sem, flat, stacked, moved
+    far_ref,
+    channel_ref,
+    own_ref,
+    other_ref,
+    sym_ref,
+    both_ref,
+    turned_ref,
+    sum_ref,
+    symbols_ref,
+    channel,
+    sems,
+    flat,
+    stacked,
+    moved,
+    stage,
 ):
-    copy = pltpu.make_async_copy(far_ref, symbols_ref, sem)
-    copy.start()
-    copy.wait()
+    copies = [
+        pltpu.make_async_copy(far_ref, symbols_ref, sems.at[0]),
+        pltpu.make_async_copy(channel_ref, channel, sems.at[1]),
+    ]
+    for copy in copies:
+        copy.start()
+    copies[0].wait()
     _, layers, parts, syms, subcarriers = symbols_ref.shape
     tiles, sub, height, _ = sym_ref.shape
     few = 32
@@ -429,6 +433,25 @@
                     piece = turn(piece, (b - k % quads) * few)
                     value = piece if b == 0 else jnp.where(lanes >= b * few, piece, value)
                 sym_ref[t, k, pl.ds(g * ROWS, ROWS), :] = value
+                both_ref[t, k, pl.ds(g * ROWS, ROWS), :] = value + pltpu.roll(
+                    value, ROWS - syms, 0
+                )
+    copies[1].wait()
+    antennas = channel.shape[1]
+    for t in range(tiles):
+        for a in range(antennas):
+            for r in range(2):
+                for h in range(layers // ROWS):
+                    stage[t, pl.ds((a * 2 + r) * layers + h * ROWS, ROWS), :] = channel[
+                        0, a, r, pl.ds(h * ROWS, ROWS), pl.ds(t * WIDE, WIDE)
+                    ]
+        for r in range(2):
+            for m in range(layers):
+                for h in range(antennas // ROWS):
+                    first = h * ROWS * 2 * layers + r * layers + m
+                    turned_ref[t, r, m, pl.ds(h * ROWS, ROWS), :] = stage[
+                        t, pl.ds(first, ROWS, stride=2 * layers), :
+                    ]
     own, other = unpacked(own_ref), unpacked(other_ref)
     for (l, h), value in own.items():
         sum_ref[pl.ds((l * 2 + h) * ROWS, ROWS), :] = value + other[l, h]
@@ -437,11 +460,11 @@
 def transmit_kernel(*refs, which, last, lanes_count, chunk):
     per_tile = WIDE // chunk
     ins, rest = refs[:per_tile], refs[per_tile:]
-    amp, chan, sym, table_ref, twist = rest[:5]
-    before = rest[5] if which else None
-    out_ref = out = rest[5 + which]
-    packs, pack, whole, norm, scale, scaled, weight, mixed, grid, table, spec_a, spec_b, sems = rest[
-        6 + which : 19 + which
+    amp, chan, sym, sums, table_ref, twist = rest[:6]
+    before = rest[6] if which else None
+    out_ref = out = rest[6 + which]
+    packs, pack, whole, norm, scale, scaled, weight, grid, table, spec_a, spec_b, sems = rest[
+        7 + which : 19 + which
     ]
     if last:
         out, out_sems = rest[19 + which :]
@@ -497,11 +520,13 @@
         whole[spot, :] = jnp.exp2(tails[0][h]) * FULL
         norm[spot, :] = jnp.exp2(-tails[1][h])
         scale[spot, :] = amp[tile, spot, :] * grow
-    for r in range(2):
-        for m in range(order):
-            for g in range(groups):
-                spot = pl.ds(g * ROWS, ROWS)
-                scaled[r, m, spot, :] = chan[tile, r, m, spot, :] * norm[pl.ds(m, 1), :]
+    for m in range(order):
+        for g in range(groups):
+            spot = pl.ds(g * ROWS, ROWS)
+            re, im = [chan[tile, r, m, spot, :] * norm[pl.ds(m, 1), :] for r in range(2)]
+            scaled[0, m, spot, :] = re
+            scaled[1, m, spot, :] = im
+            scaled[2, m, spot, :] = re - im
 
     def row(l, m):
         return pack[pl.ds(l * order + m, 1), :]
@@ -514,48 +539,57 @@
 
         for m in range(order):
             here = [
-                [scaled[r, m, pl.ds(g * ROWS, ROWS), :] for g in range(groups)] for r in range(2)
+                [scaled[r, m, pl.ds(g * ROWS, ROWS), :] for g in range(groups)] for r in range(3)
             ]
             for l in range(base, base + 4):
-                inv_re = row(min(l, m), max(l, m)) if l != m else whole[pl.ds(l, 1), :]
-                inv_im = row(max(l, m), min(l, m)) if l != m else None
+                if l == m:
+                    inv = whole[pl.ds(l, 1), :]
+                    for g in range(groups):
+                        add((l, 0, g), here[0][g] * inv)
+                        add((l, 2, g), here[2][g] * inv)
+                    continue
+                inv_re, inv_im = row(min(l, m), max(l, m)), row(max(l, m), min(l, m))
                 if l > m:
                     inv_im = -inv_im
+                total = inv_re + inv_im
                 for g in range(groups):
-                    re, im = here[0][g], here[1][g]
-                    if inv_im is None:
-                        add((l, 0, g), re * inv_re)
-                        add((l, 1, g), -(im * inv_re))
-                    else:
-                        add((l, 0, g), re * inv_re + im * inv_im)
-                        add((l, 1, g), re * inv_im - im * inv_re)
-        for (l, r, g), value in acc.items():
-            value = value * scale[pl.ds(l, 1), :]
-            weight[r, l, pl.ds(g * ROWS, ROWS), :] = value.astype(jnp.bfloat16).astype(jnp.float32)
+                    add((l, 0, g), here[0][g] * inv_re)
+                    add((l, 1, g), here[1][g] * inv_im)
+                    add((l, 2, g), here[2][g] * total)
+        for l in range(base, base + 4):
+            for g in range(groups):
+                first, second, third = [acc[l, i, g] for i in range(3)]
+                grown = scale[pl.ds(l, 1), :]
+                spot = pl.ds(g * ROWS, ROWS)
+                re = ((first + second) * grown).astype(jnp.bfloat16).astype(jnp.float32)
+                im = ((third - first + second) * grown).astype(jnp.bfloat16).astype(jnp.float32)
+                weight[0, l, spot, :] = re
+                weight[1, l, spot, :] = im
+                weight[2, l, spot, :] = re + im
 
     def precode(k, carry):
         acc = {}
         for l in range(order):
-            w_re = [weight[0, l, pl.ds(g * ROWS, ROWS), :] for g in range(groups)]
-            w_im = [weight[1, l, pl.ds(g * ROWS, ROWS), :] for g in range(groups)]
+            held = [
+                [weight[i, l, pl.ds(g * ROWS, ROWS), :] for g in range(groups)] for i in range(3)
+            ]
             for s in range(syms):
-                s_re = sym[tile, k, pl.ds((l * 2 + 0) * syms + s, 1), :]
-                s_im = sym[tile, k, pl.ds((l * 2 + 1) * syms + s, 1), :]
-                for g in range(groups):
-                    re = w_re[g] * s_re - w_im[g] * s_im
-                    im = w_re[g] * s_im + w_im[g] * s_re
-                    if l == 0:
-                        acc[s, g] = (re, im)
-                    else:
-                        old = acc[s, g]
-                        acc[s, g] = (old[0] + re, old[1] + im)
+                parts = (
+                    sym[tile, k, pl.ds(l * 2 * syms + s, 1), :],
+                    sym[tile, k, pl.ds((l * 2 + 1) * syms + s, 1), :],
+                    sums[tile, k, pl.ds(l * 2 * syms + s, 1), :],
+                )
+                for i in range(3):
+                    for g in range(groups):
+                        term = held[i][g] * parts[i]
+                        acc[s, g, i] = term if l == 0 else acc[s, g, i] + term
         for r in range(2):
+            values = []
             for s in range(syms):
                 for g in range(groups):
-                    spot = pl.ds(g * ROWS * syms + s, ROWS, stride=syms)
-                    mixed[r, spot, :] = acc[s, g][r]
-        for r in range(2):
-            exact = mixed[r]
+                    first, second, third = [acc[s, g, i] for i in range(3)]
+                    values.append(first - second if r == 0 else third - first - second)
+            exact = jnp.concatenate(values, axis=0)
             high = exact.astype(jnp.bfloat16)
             grid[k, :, pl.ds(r * WIDE, WIDE)] = high
             grid[k, :, pl.ds((2 + r) * WIDE, WIDE)] = (exact - high.astype(jnp.float32)).astype(
@@ -598,13 +632,18 @@
                 (even_re - odd_re, even_im - odd_im),
                 (gap_re + far_im, gap_im - far_re),
             )
-            spot = pl.ds(g * ROWS, ROWS)
+            s, first = g // groups, g % groups * ROWS
             for q, pair in enumerate(outs):
                 for r in range(2):
                     value = pair[r]
+                    spot = pl.ds(g * ROWS, ROWS)
                     if which:
                         value = value + before[n, q, r, spot, :]
-                    out[n, q, r, spot, :] = value
+                    if last:
+                        start = (first * 2 + r) * syms + s
+                        out[n, q, pl.ds(start, ROWS, stride=2 * syms), :] = value
+                    else:
+                        out[n, q, r, spot, :] = value
 
     done = []
     product(0)
@@ -615,14 +654,13 @@
         if not last:
             continue
         for q in range(4):
-            for r in range(2):
-                copy = pltpu.make_async_copy(
-                    out.at[n, q, r].reshape(antennas, syms, WIDE),
-                    out_ref.at[:, r, q * count + n],
-                    out_sems.at[n, q, r],
-                )
-                copy.start()
-                done.append(copy)
+            copy = pltpu.make_async_copy(
+                out.at[n, q].reshape(antennas, 2, syms, WIDE),
+                out_ref.at[:, :, q * count + n],
+                out_sems.at[n, q],
+            )
+            copy.start()
+            done.append(copy)
     for copy in done:
         copy.wait()
 
@@ -675,14 +713,13 @@
     table, twist = jnp.asarray(table), jnp.asarray(twist)
     dma = pltpu.SemaphoreType.DMA
 
-    amp, own, mix, turned, *pieces = pl.pallas_call(
+    amp, own, mix, *pieces = pl.pallas_call(
         functools.partial(gram_kernel, lanes=lanes, chunk=chunk),
         out_shape=[pltpu.VMEM((tiles, order, WIDE), f32)]
         + [pltpu.VMEM((cells, 1, WIDE), f32)] * 2
-        + [pltpu.VMEM((tiles, 2, order, antennas, WIDE), f32)]
         + [pltpu.VMEM((order * ROWS + order, WIDE), jnp.int16)] * lanes,
         in_specs=[HBM] * 6,
-        out_specs=[VMEM] * (4 + lanes),
+        out_specs=[VMEM] * (3 + lanes),
         scratch_shapes=[
             pltpu.VMEM((antennas, 2, order, blocks), f32),
             pltpu.VMEM((1, blocks), jnp.int32),
@@ -692,7 +729,6 @@
             pltpu.SMEM(coupling.shape, f32),
             pltpu.VMEM((lanes, order * ROWS + order, WIDE), jnp.int16),
             pltpu.VMEM((order, WIDE), f32),
-            pltpu.VMEM((tiles, antennas * 2 * order, WIDE), f32),
             dma((5 + tiles,)),
         ],
         compiler_params=params(16),
@@ -701,26 +737,30 @@
     parts = swap(pieces)
     transmit = lax.all_to_all(own, "cell", 0, 0, tiled=True)
 
-    sym, pair = pl.pallas_call(
+    sym, both, turned, pair = pl.pallas_call(
         arrange_kernel,
         out_shape=(
             pltpu.VMEM((tiles, sub, order * 2 * syms, WIDE), f32),
+            pltpu.VMEM((tiles, sub, order * 2 * syms, WIDE), f32),
+            pltpu.VMEM((tiles, 2, order, antennas, WIDE), f32),
             pltpu.VMEM((order * ROWS, WIDE), f32),
         ),
-        in_specs=[HBM, VMEM, VMEM],
-        out_specs=(VMEM, VMEM),
+        in_specs=[HBM, HBM, VMEM, VMEM],
+        out_specs=(VMEM,) * 4,
         scratch_shapes=[
             pltpu.VMEM(symbols.shape, bf16),
-            pltpu.SemaphoreType.DMA,
+            pltpu.VMEM(channel.shape, f32),
+            dma((2,)),
             pltpu.VMEM((order * 2 * syms, subcarriers), f32),
             pltpu.VMEM((subcarriers // (sub * 32) * order * 2 * syms, sub * 32), bf16),
             pltpu.VMEM((subcarriers // (sub * 32) * order * 2 * syms, sub * 32), f32),
+            pltpu.VMEM((tiles, antennas * 2 * order, WIDE), f32),
         ],
         compiler_params=params(16),
         cost_estimate=pl.CostEstimate(flops=10**9, bytes_accessed=8 * 10**6, transcendentals=0),
         name="arrange",
-    )(far(symbols), near(parts[0]), near(parts[lanes // 2]))
-    parts = [pair] + [part for s, part in enumerate(parts) if s not in (0, lanes // 2)]
+    )(far(symbols), far(channel), near(parts[0]), near(parts[lanes - 1]))
+    parts = [pair] + parts[1 : lanes - 1]
 
     packed = pl.pallas_call(
         functools.partial(solve_kernel, count=lanes - 1),
@@ -747,7 +787,7 @@
                 transmit_kernel, which=which, last=last, lanes_count=lanes, chunk=chunk
             ),
             out_shape=[shape(final, f32) if last else pltpu.VMEM(result, f32)],
-            in_specs=[VMEM] * (per_tile + 3) + [HBM, VMEM] + [VMEM] * which,
+            in_specs=[VMEM] * (per_tile + 4) + [HBM, VMEM] + [VMEM] * which,
             out_specs=[HBM if last else VMEM],
             scratch_shapes=[
                 pltpu.VMEM((per_tile, order * ROWS + 2 * order, WIDE), jnp.int16),
@@ -755,16 +795,15 @@
                 pltpu.VMEM((order, WIDE), f32),
                 pltpu.VMEM((order, WIDE), f32),
                 pltpu.VMEM((order, WIDE), f32),
-                pltpu.VMEM((2, order, antennas, WIDE), f32),
-                pltpu.VMEM((2, order, antennas, WIDE), f32),
-                pltpu.VMEM((2, height, WIDE), f32),
+                pltpu.VMEM((3, order, antennas, WIDE), f32),
+                pltpu.VMEM((3, order, antennas, WIDE), f32),
                 pltpu.VMEM((sub, height, 4 * WIDE), bf16),
                 pltpu.VMEM((count, 4 * WIDE, 2 * WIDE), bf16),
                 pltpu.VMEM((sub * height, 2 * WIDE), f32),
                 pltpu.VMEM((sub * height, 2 * WIDE), f32),
                 dma((2,)),
             ]
-            + [pltpu.VMEM(result, f32), dma((count, 4, 2))] * last,
+            + [pltpu.VMEM((count, 4, 2 * height, WIDE), f32), dma((count, 4))] * last,
             compiler_params=params(16),
             cost_estimate=pl.CostEstimate(
                 flops=10**9, bytes_accessed=4 * 10**6, transcendentals=0
@@ -775,6 +814,7 @@
             near(amp),
             near(turned),
             near(sym),
+            near(both),
             far(table),
             near(twist),
             *map(near, out),

time: 33.8 us -> 32.5 us (0.962)
  waiting for transfers between devices: 4.8 us -> 3.03 us
  starting transfers between devices: 13.2 us -> 14 us
    ppermute x6, waiting for transfers between devices: 4.17 us -> 1.75 us  [swap(): lax.ppermute(pieces[s], 'lane', [(j, j ^ s) for j in range(lanes)])]
    ppermute x6, starting transfers between devices: 9.45 us -> 10.3 us  [swap(): lax.ppermute(pieces[s], 'lane', [(j, j ^ s) for j in range(lanes)])]
    all_to_all x1, waiting for transfers between devices: 0.63 us -> 1.27 us  [per_device(): transmit = lax.all_to_all(own, 'cell', 0, 0, tiled=True)]
    pallas_call x2, Pallas kernels: 6.85 us -> 6.44 us  [per_device(): pl.pallas_call(functools.partial(transmit_kernel, which=which, last=last,...]
    pallas_call x1, Pallas kernels: 2.14 us -> 2.52 us  [per_device(): pl.pallas_call(arrange_kernel, out_shape=(pltpu.VMEM((tiles, sub, order *...]
  transfers between devices with their start and end apart: 7 -> 7, of which waited for: 3 -> 3; matrix products, arithmetic and copies ran while one was open for 0% -> 0% of each run, Pallas kernels for 15% -> 16%
where the time goes in v3:
time: 32.5 us; the launch traced here: 32.3 us
  Pallas kernels  15.2 us (47%)
  starting transfers between devices  14 us (43%)
  waiting for transfers between devices  3.03 us (9%)
    ppermute x6, starting transfers between devices, swap(): lax.ppermute(pieces[s], 'lane', [(j, j ^ s) for j in range(lanes)])  10.3 us
    pallas_call x2, Pallas kernels, per_device(): pl.pallas_call(functools.partial(transmit_kernel, which=which, last=last,...  6.44 us
    all_to_all x1, starting transfers between devices, per_device(): transmit = lax.all_to_all(own, 'cell', 0, 0, tiled=True)  3.72 us
    pallas_call x1, Pallas kernels, per_device(): pl.pallas_call(functools.partial(solve_kernel, count=lanes - 1), out_shap...  3.4 us
    pallas_call x1, Pallas kernels, per_device(): pl.pallas_call(functools.partial(gram_kernel, lanes=lanes, chunk=chunk),...  2.83 us
    pallas_call x1, Pallas kernels, per_device(): pl.pallas_call(arrange_kernel, out_shape=(pltpu.VMEM((tiles, sub, order *...  2.52 us
    ppermute x6, waiting for transfers between devices, swap(): lax.ppermute(pieces[s], 'lane', [(j, j ^ s) for j in range(lanes)])  1.75 us
    all_to_all x1, waiting for transfers between devices, per_device(): transmit = lax.all_to_all(own, 'cell', 0, 0, tiled=True)  1.27 us
  transfers between devices with their start and end apart: 7, of which 3 were waited for; matrix products, arithmetic and copies ran while one was open for 0% of the time, Pallas kernels for 16%

profile of v3, /device:TPU:0, one launch (start us, length us, event | category | flops | bytes accessed | tf_op | source)
XLA Modules:
  0.0 32.3 jit_solution(3892140180189928443)
XLA Ops:
  0.0 0.0 copy-start
  0.0 2.8 %gram.1 = (f32[2,16,128]{2,1,0:T(8,128)S(1)}, f32[8,1,128]{2,1,0:T(1,128)}, f32[8,1,128]{2,1,0:T(1,128)S(1)}, s16[144,128]{1,0:T(8,128)(2,1)S(1)}, s16[144,128]{...) custom-call(f32[1,16,2,16,256]{4,3,2,1,0:T(8,128)} %channel_ref.1, s32[1,256]{1,0:T(1,128)} %refs_1_.1, ...), custom_call_target="tpu_custom_call" | custom-call | tf_op jit(solution)/shard_map/gram/pallas_call | solution.py:716
  2.8 5.1 %collective-permute-start = (s16[144,128]{1,0:T(8,128)(2,1)S(1)}, s16[144,128]{1,0:T(8,128)(2,1)S(1)}, u32[]{:S(2)}, u32[]{:S(2)}) collective-permute-start(s16[144,128]{1,0:T(8,128)(2,1)S(1)} %get-tuple-element.19), channel_id=1, source_target_pairs={{0,3},{1,2},{2,1},{3,0},{4,7},{5,6},{6,5},{7,4},{8,11},{9,10},{10,... | collective-permute-start | bytes 110600 | tf_op jit(solution)/shard_map/ppermute | solution.py:698
  8.0 3.7 %all-to-all-start = ((f32[8,1,128]{2,1,0:T(1,128)}), f32[8,1,128]{2,1,0:T(1,128)S(1)}, u32[]{:S(2)}, u32[]{:S(2)}) async-start(f32[8,1,128]{2,1,0:T(1,128)} %get-tuple-element.16), calls=%async_computation | async-start | bytes 8192 | tf_op jit(solution)/shard_map/all_to_all | solution.py:738
  11.7 0.0 collective-permute-start.1
  11.7 0.8 %collective-permute-start.2 = (s16[144,128]{1,0:T(8,128)(2,1)S(1)}, s16[144,128]{1,0:T(8,128)(2,1)S(1)}, u32[]{:S(2)}, u32[]{:S(2)}) collective-permute-start(s16[144,128]{1,0:T(8,128)(2,1)S(1)} %get-tuple-element.22), channel_id=1, source_target_pairs={{0,2},{1,3},{2,0},{3,1},{4,6},{5,7},{6,4},{7,5},{8,10},{9,11},{10,... | collective-permute-start | bytes 110600 | tf_op jit(solution)/shard_map/ppermute | solution.py:698
  12.5 0.0 collective-permute-done.other_ref
  12.5 2.5 %arrange.1 = (f32[2,12,64,128]{3,2,1,0:T(8,128)S(1)}, f32[2,12,64,128]{3,2,1,0:T(8,128)S(1)}, f32[2,2,16,16,128]{4,3,2,1,0:T(8,128)S(1)}, f32[128,128]{1,0:T(8,128)S(1)}) custom-call(bf16[1,16,2,2,3072]{4,3,2,1,0:T(2,128)(2,1)} %far_ref.1, f32[1,16,2,16,256]{4,3,2,1,0:T(8,128)} %channel_ref.1, s16[144,128]{1,0:T(8,128)(2,1)S(1)} %get-tuple-element.18.own_ref, ...), custom_call_target="tpu_custom_call" | custom-call | flops 1000000000 | bytes 8000000 | tf_op jit(solution)/shard_map/arrange/pallas_call | solution.py:740
  15.0 1.3 %all-to-all-done.refs_0_ = f32[8,1,128]{2,1,0:T(1,128)S(1)} async-done(((f32[8,1,128]{2,1,0:T(1,128)}), f32[8,1,128]{2,1,0:T(1,128)S(1)}, u32[]{:S(2)}, u32[]{:S(2)}) %all-to-all-start) | async-done | bytes 4128 | tf_op jit(solution)/shard_map/all_to_all | solution.py:738
  16.3 0.0 collective-permute-done.1.refs_3_
  16.3 0.3 %collective-permute-done.2.refs_4_ = s16[144,128]{1,0:T(8,128)(2,1)S(1)} collective-permute-done((s16[144,128]{1,0:T(8,128)(2,1)S(1)}, s16[144,128]{1,0:T(8,128)(2,1)S(1)}, u32[]{:S(2)}, u32[]{:S(2)}) %collective-permute-start.2) | collective-permute-done | bytes 36896 | tf_op jit(solution)/shard_map/ppermute | solution.py:698
  16.6 3.4 %solve.1.refs_0_ = s16[160,128]{1,0:T(8,128)(2,1)S(1)} custom-call(f32[8,1,128]{2,1,0:T(1,128)S(1)} %all-to-all-done.refs_0_, f32[8,1,128]{2,1,0:T(1,128)S(1)} %get-tuple-element.17.refs_1_, f32[128,128]{1,0:T(8,128)S(1)} %get-tuple-element.20.refs_2_, s16[144,128]{1,0:T(8,128)(2,1)S(1)} %collective-permute-done.1.refs_3_, ...), custom_call_target="tpu_custom_call" | custom-call | tf_op jit(solution)/shard_map/solve/pallas_call | solution.py:765
  20.0 1.1 %collective-permute-start.5 = (s16[160,128]{1,0:T(8,128)(2,1)S(1)}, s16[160,128]{1,0:T(8,128)(2,1)S(1)}, u32[]{:S(2)}, u32[]{:S(2)}) collective-permute-start(s16[160,128]{1,0:T(8,128)(2,1)S(1)} %solve.1.refs_0_), channel_id=1, source_target_pairs={{0,2},{1,3},{2,0},{3,1},{4,6},{5,7},{6,4},{7,5},{8,10},{9,11},{10,... | collective-permute-start | bytes 122888 | tf_op jit(solution)/shard_map/ppermute | solution.py:698
  21.1 3.3 %collective-permute-start.4 = (s16[160,128]{1,0:T(8,128)(2,1)S(1)}, s16[160,128]{1,0:T(8,128)(2,1)S(1)}, u32[]{:S(2)}, u32[]{:S(2)}) collective-permute-start(s16[160,128]{1,0:T(8,128)(2,1)S(1)} %solve.1.refs_0_), channel_id=1, source_target_pairs={{0,3},{1,2},{2,1},{3,0},{4,7},{5,6},{6,5},{7,4},{8,11},{9,10},{10,... | collective-permute-start | bytes 122888 | tf_op jit(solution)/shard_map/ppermute | solution.py:698
  24.4 0.0 collective-permute-start.3
  24.4 1.4 %collective-permute-done.5.refs_1_ = s16[160,128]{1,0:T(8,128)(2,1)S(1)} collective-permute-done((s16[160,128]{1,0:T(8,128)(2,1)S(1)}, s16[160,128]{1,0:T(8,128)(2,1)S(1)}, u32[]{:S(2)}, u32[]{:S(2)}) %collective-permute-start.5) | collective-permute-done | bytes 40992 | tf_op jit(solution)/shard_map/ppermute | solution.py:698
  25.8 0.0 copy-done
  25.8 2.7 %transmit.2.refs_8_ = f32[8,4,2,32,128]{4,3,2,1,0:T(8,128)S(1)} custom-call(s16[160,128]{1,0:T(8,128)(2,1)S(1)} %solve.1.refs_0_, s16[160,128]{1,0:T(8,128)(2,1)S(1)} %collective-permute-done.5.refs_1_, f32[2,16,128]{2,1,0:T(8,128)S(1)} %get-tuple-element.23.refs_2_, f32[2,2,16,16,128]{4,3,2,1,0:T(8,128)S(1)} %get-tuple-element.24.refs_3_, ...), custom_call_target="tpu_custom_call" | custom-call | flops 1000000000 | bytes 4000000 | tf_op jit(solution)/shard_map/transmit/pallas_call | solution.py:785
  28.5 0.0 collective-permute-done.4.refs_1_
  28.5 0.0 collective-permute-done.3.refs_0_
  28.5 3.8 %transmit.3 = f32[16,2,32,2,128]{4,3,2,1,0:T(2,128)} custom-call(s16[160,128]{1,0:T(8,128)(2,1)S(1)} %collective-permute-done.3.refs_0_, s16[160,128]{1,0:T(8,128)(2,1)S(1)} %collective-permute-done.4.refs_1_, f32[2,16,128]{2,1,0:T(8,128)S(1)} %get-tuple-element.23.refs_2_, f32[2,2,16,16,128]{4,3,2,1,0:T(8,128)S(1)} %get-tuple-element.24.refs_3_, ...), custom_call_target="tpu_custom_call" | custom-call | flops 1000000000 | bytes 4000000 | tf_op jit(solution)/shard_map/transmit/pallas_call | solution.py:785
Async XLA Ops:
  0.0 25.8 %copy-start = (f32[8,24,128]{2,1,0:T(8,128)S(1)}, f32[8,24,128]{2,1,0:T(8,128)}, u32[]{:S(2)}) copy-start(f32[8,24,128]{2,1,0:T(8,128)} %constant.5.clone.refs_7_) | copy-start | bytes 294916
  2.8 9.6 %collective-permute-start = (s16[144,128]{1,0:T(8,128)(2,1)S(1)}, s16[144,128]{1,0:T(8,128)(2,1)S(1)}, u32[]{:S(2)}, u32[]{:S(2)}) collective-permute-start(s16[144,128]{1,0:T(8,128)(2,1)S(1)} %get-tuple-element.19), channel_id=1, source_target_pairs={{0,3},{1,2},{2,1},{3,0},{4,7},{5,6},{6,5},{7,4},{8,11},{9,10},{10,... | collective-permute-start | bytes 110600 | tf_op jit(solution)/shard_map/ppermute | solution.py:698
  8.0 8.3 %all-to-all-start = ((f32[8,1,128]{2,1,0:T(1,128)}), f32[8,1,128]{2,1,0:T(1,128)S(1)}, u32[]{:S(2)}, u32[]{:S(2)}) async-start(f32[8,1,128]{2,1,0:T(1,128)} %get-tuple-element.16), calls=%async_computation | async-start | bytes 8192 | tf_op jit(solution)/shard_map/all_to_all | solution.py:738
  11.7 4.6 %collective-permute-start.1 = (s16[144,128]{1,0:T(8,128)(2,1)S(1)}, s16[144,128]{1,0:T(8,128)(2,1)S(1)}, u32[]{:S(2)}, u32[]{:S(2)}) collective-permute-start(s16[144,128]{1,0:T(8,128)(2,1)S(1)} %get-tuple-element.21), channel_id=1, source_target_pairs={{0,1},{1,0},{2,3},{3,2},{4,5},{5,4},{6,7},{7,6},{8,9},{9,8},{10,11... | collective-permute-start | bytes 110600 | tf_op jit(solution)/shard_map/ppermute | solution.py:698
  11.7 4.9 %collective-permute-start.2 = (s16[144,128]{1,0:T(8,128)(2,1)S(1)}, s16[144,128]{1,0:T(8,128)(2,1)S(1)}, u32[]{:S(2)}, u32[]{:S(2)}) collective-permute-start(s16[144,128]{1,0:T(8,128)(2,1)S(1)} %get-tuple-element.22), channel_id=1, source_target_pairs={{0,2},{1,3},{2,0},{3,1},{4,6},{5,7},{6,4},{7,5},{8,10},{9,11},{10,... | collective-permute-start | bytes 110600 | tf_op jit(solution)/shard_map/ppermute | solution.py:698
  20.0 5.8 %collective-permute-start.5 = (s16[160,128]{1,0:T(8,128)(2,1)S(1)}, s16[160,128]{1,0:T(8,128)(2,1)S(1)}, u32[]{:S(2)}, u32[]{:S(2)}) collective-permute-start(s16[160,128]{1,0:T(8,128)(2,1)S(1)} %solve.1.refs_0_), channel_id=1, source_target_pairs={{0,2},{1,3},{2,0},{3,1},{4,6},{5,7},{6,4},{7,5},{8,10},{9,11},{10,... | collective-permute-start | bytes 122888 | tf_op jit(solution)/shard_map/ppermute | solution.py:698
  21.1 7.4 %collective-permute-start.4 = (s16[160,128]{1,0:T(8,128)(2,1)S(1)}, s16[160,128]{1,0:T(8,128)(2,1)S(1)}, u32[]{:S(2)}, u32[]{:S(2)}) collective-permute-start(s16[160,128]{1,0:T(8,128)(2,1)S(1)} %solve.1.refs_0_), channel_id=1, source_target_pairs={{0,3},{1,2},{2,1},{3,0},{4,7},{5,6},{6,5},{7,4},{8,11},{9,10},{10,... | collective-permute-start | bytes 122888 | tf_op jit(solution)/shard_map/ppermute | solution.py:698
  24.4 4.1 %collective-permute-start.3 = (s16[160,128]{1,0:T(8,128)(2,1)S(1)}, s16[160,128]{1,0:T(8,128)(2,1)S(1)}, u32[]{:S(2)}, u32[]{:S(2)}) collective-permute-start(s16[160,128]{1,0:T(8,128)(2,1)S(1)} %solve.1.refs_0_), channel_id=1, source_target_pairs={{0,1},{1,0},{2,3},{3,2},{4,5},{5,4},{6,7},{7,6},{8,9},{9,8},{10,11... | collective-permute-start | bytes 122888 | tf_op jit(solution)/shard_map/ppermute | solution.py:698

commit v4 on v3

--- a/solution.py
+++ b/solution.py
@@ -317,14 +317,49 @@
             for l in range(ROWS, order):
                 ref[at(l, 0), :] = -sign * ref[column(l, 0), :]
 
+    def pair(error, squared, total, grown):
+        for l in range(order):
+            for h in range(2):
+                value, other = error[at(l, h), :], total[at(l, h), :]
+                value = value + pltpu.roll(value, HALF, 1)
+                d_re[at(l, h), :] = value
+                d_im[at(l, h), :] = jnp.where(low, value, other + pltpu.roll(other, HALF, 1))
+        for base in range(0, order, 2):
+            halves = (0, 1) if base < ROWS else (1,)
+            acc = {}
+            for k in range(order):
+                right = [
+                    (i, h, ref[at(k, h), :])
+                    for i, ref in enumerate((error, total, d_im))
+                    for h in halves
+                ]
+                for l in (base, base + 1):
+                    left = row(error, l, k)
+                    lefts = (left, left, row(d_re, l, k))
+                    for i, h, value in right:
+                        term = lefts[i] * value
+                        acc[l, i, h] = acc[l, i, h] + term if k else term
+            for l in (base, base + 1):
+                for h in halves:
+                    first, second, third = [acc[l, i, h] for i in range(3)]
+                    other = pltpu.roll(first, HALF, 1)
+                    squared[at(l, h), :] = jnp.where(
+                        low, first - other, pltpu.roll(third, HALF, 1) - first - other
+                    )
+                    other = pltpu.roll(second, HALF, 1)
+                    grown[at(l, h), :] = total[at(l, h), :] + jnp.where(
+                        low, second - other, third - second - other
+                    )
+        for ref in (squared, grown):
+            for l in range(ROWS, order):
+                ref[at(l, 0), :] = -sign * ref[column(l, 0), :]
+
     spread(e_a)
     products([(e_a, e_b, None)])
 
     def two_steps(_, carry):
-        spread(e_b)
-        products([(e_b, e_a, None), (s_a, s_b, s_a)])
-        spread(e_a)
-        products([(e_a, e_b, None), (s_b, s_a, s_b)])
+        pair(e_b, e_a, s_a, s_b)
+        pair(e_a, e_b, s_b, s_a)
         return carry
 
     lax.fori_loop(0, (NS_STEPS - 2) // 2, two_steps, 0)

time: 32.5 us -> 32.4 us (level)
  no operation moved by 1% of the time
where the time goes in v4:
time: 32.4 us; the launch traced here: 32.2 us
  Pallas kernels  15.1 us (47%)
  starting transfers between devices  14 us (43%)
  waiting for transfers between devices  3.03 us (9%)
    ppermute x6, starting transfers between devices, swap(): lax.ppermute(pieces[s], 'lane', [(j, j ^ s) for j in range(lanes)])  10.3 us
    pallas_call x2, Pallas kernels, per_device(): pl.pallas_call(functools.partial(transmit_kernel, which=which, last=last,...  6.44 us
    all_to_all x1, starting transfers between devices, per_device(): transmit = lax.all_to_all(own, 'cell', 0, 0, tiled=True)  3.72 us
    pallas_call x1, Pallas kernels, per_device(): pl.pallas_call(functools.partial(solve_kernel, count=lanes - 1), out_shap...  3.29 us
    pallas_call x1, Pallas kernels, per_device(): pl.pallas_call(functools.partial(gram_kernel, lanes=lanes, chunk=chunk),...  2.83 us
    pallas_call x1, Pallas kernels, per_device(): pl.pallas_call(arrange_kernel, out_shape=(pltpu.VMEM((tiles, sub, order *...  2.52 us
    ppermute x6, waiting for transfers between devices, swap(): lax.ppermute(pieces[s], 'lane', [(j, j ^ s) for j in range(lanes)])  1.75 us
    all_to_all x1, waiting for transfers between devices, per_device(): transmit = lax.all_to_all(own, 'cell', 0, 0, tiled=True)  1.27 us
  transfers between devices with their start and end apart: 7, of which 3 were waited for; matrix products, arithmetic and copies ran while one was open for 0% of the time, Pallas kernels for 16%

profile of v4, /device:TPU:0, one launch (start us, length us, event | category | flops | bytes accessed | tf_op | source)
XLA Modules:
  0.0 32.2 jit_solution(10384327662220269755)
XLA Ops:
  0.0 0.0 copy-start
  0.0 2.8 %gram.1 = (f32[2,16,128]{2,1,0:T(8,128)S(1)}, f32[8,1,128]{2,1,0:T(1,128)}, f32[8,1,128]{2,1,0:T(1,128)S(1)}, s16[144,128]{1,0:T(8,128)(2,1)S(1)}, s16[144,128]{...) custom-call(f32[1,16,2,16,256]{4,3,2,1,0:T(8,128)} %channel_ref.1, s32[1,256]{1,0:T(1,128)} %refs_1_.1, ...), custom_call_target="tpu_custom_call" | custom-call | tf_op jit(solution)/shard_map/gram/pallas_call | solution.py:751
  2.8 5.1 %collective-permute-start = (s16[144,128]{1,0:T(8,128)(2,1)S(1)}, s16[144,128]{1,0:T(8,128)(2,1)S(1)}, u32[]{:S(2)}, u32[]{:S(2)}) collective-permute-start(s16[144,128]{1,0:T(8,128)(2,1)S(1)} %get-tuple-element.19), channel_id=1, source_target_pairs={{0,3},{1,2},{2,1},{3,0},{4,7},{5,6},{6,5},{7,4},{8,11},{9,10},{10,... | collective-permute-start | bytes 110600 | tf_op jit(solution)/shard_map/ppermute | solution.py:733
  8.0 3.7 %all-to-all-start = ((f32[8,1,128]{2,1,0:T(1,128)}), f32[8,1,128]{2,1,0:T(1,128)S(1)}, u32[]{:S(2)}, u32[]{:S(2)}) async-start(f32[8,1,128]{2,1,0:T(1,128)} %get-tuple-element.16), calls=%async_computation | async-start | bytes 8192 | tf_op jit(solution)/shard_map/all_to_all | solution.py:773
  11.7 0.0 collective-permute-start.1
  11.7 0.8 %collective-permute-start.2 = (s16[144,128]{1,0:T(8,128)(2,1)S(1)}, s16[144,128]{1,0:T(8,128)(2,1)S(1)}, u32[]{:S(2)}, u32[]{:S(2)}) collective-permute-start(s16[144,128]{1,0:T(8,128)(2,1)S(1)} %get-tuple-element.22), channel_id=1, source_target_pairs={{0,2},{1,3},{2,0},{3,1},{4,6},{5,7},{6,4},{7,5},{8,10},{9,11},{10,... | collective-permute-start | bytes 110600 | tf_op jit(solution)/shard_map/ppermute | solution.py:733
  12.5 0.0 collective-permute-done.other_ref
  12.5 2.5 %arrange.1 = (f32[2,12,64,128]{3,2,1,0:T(8,128)S(1)}, f32[2,12,64,128]{3,2,1,0:T(8,128)S(1)}, f32[2,2,16,16,128]{4,3,2,1,0:T(8,128)S(1)}, f32[128,128]{1,0:T(8,128)S(1)}) custom-call(bf16[1,16,2,2,3072]{4,3,2,1,0:T(2,128)(2,1)} %far_ref.1, f32[1,16,2,16,256]{4,3,2,1,0:T(8,128)} %channel_ref.1, s16[144,128]{1,0:T(8,128)(2,1)S(1)} %get-tuple-element.18.own_ref, ...), custom_call_target="tpu_custom_call" | custom-call | flops 1000000000 | bytes 8000000 | tf_op jit(solution)/shard_map/arrange/pallas_call | solution.py:775
  15.0 1.3 %all-to-all-done.refs_0_ = f32[8,1,128]{2,1,0:T(1,128)S(1)} async-done(((f32[8,1,128]{2,1,0:T(1,128)}), f32[8,1,128]{2,1,0:T(1,128)S(1)}, u32[]{:S(2)}, u32[]{:S(2)}) %all-to-all-start) | async-done | bytes 4128 | tf_op jit(solution)/shard_map/all_to_all | solution.py:773
  16.3 0.0 collective-permute-done.1.refs_3_
  16.3 0.3 %collective-permute-done.2.refs_4_ = s16[144,128]{1,0:T(8,128)(2,1)S(1)} collective-permute-done((s16[144,128]{1,0:T(8,128)(2,1)S(1)}, s16[144,128]{1,0:T(8,128)(2,1)S(1)}, u32[]{:S(2)}, u32[]{:S(2)}) %collective-permute-start.2) | collective-permute-done | bytes 36896 | tf_op jit(solution)/shard_map/ppermute | solution.py:733
  16.6 3.3 %solve.1.refs_0_ = s16[160,128]{1,0:T(8,128)(2,1)S(1)} custom-call(f32[8,1,128]{2,1,0:T(1,128)S(1)} %all-to-all-done.refs_0_, f32[8,1,128]{2,1,0:T(1,128)S(1)} %get-tuple-element.17.refs_1_, f32[128,128]{1,0:T(8,128)S(1)} %get-tuple-element.20.refs_2_, s16[144,128]{1,0:T(8,128)(2,1)S(1)} %collective-permute-done.1.refs_3_, ...), custom_call_target="tpu_custom_call" | custom-call | tf_op jit(solution)/shard_map/solve/pallas_call | solution.py:800
  19.9 1.1 %collective-permute-start.5 = (s16[160,128]{1,0:T(8,128)(2,1)S(1)}, s16[160,128]{1,0:T(8,128)(2,1)S(1)}, u32[]{:S(2)}, u32[]{:S(2)}) collective-permute-start(s16[160,128]{1,0:T(8,128)(2,1)S(1)} %solve.1.refs_0_), channel_id=1, source_target_pairs={{0,2},{1,3},{2,0},{3,1},{4,6},{5,7},{6,4},{7,5},{8,10},{9,11},{10,... | collective-permute-start | bytes 122888 | tf_op jit(solution)/shard_map/ppermute | solution.py:733
  21.0 3.3 %collective-permute-start.4 = (s16[160,128]{1,0:T(8,128)(2,1)S(1)}, s16[160,128]{1,0:T(8,128)(2,1)S(1)}, u32[]{:S(2)}, u32[]{:S(2)}) collective-permute-start(s16[160,128]{1,0:T(8,128)(2,1)S(1)} %solve.1.refs_0_), channel_id=1, source_target_pairs={{0,3},{1,2},{2,1},{3,0},{4,7},{5,6},{6,5},{7,4},{8,11},{9,10},{10,... | collective-permute-start | bytes 122888 | tf_op jit(solution)/shard_map/ppermute | solution.py:733
  24.3 0.0 collective-permute-start.3
  24.3 1.4 %collective-permute-done.5.refs_1_ = s16[160,128]{1,0:T(8,128)(2,1)S(1)} collective-permute-done((s16[160,128]{1,0:T(8,128)(2,1)S(1)}, s16[160,128]{1,0:T(8,128)(2,1)S(1)}, u32[]{:S(2)}, u32[]{:S(2)}) %collective-permute-start.5) | collective-permute-done | bytes 40992 | tf_op jit(solution)/shard_map/ppermute | solution.py:733
  25.7 0.0 copy-done
  25.7 2.7 %transmit.2.refs_8_ = f32[8,4,2,32,128]{4,3,2,1,0:T(8,128)S(1)} custom-call(s16[160,128]{1,0:T(8,128)(2,1)S(1)} %solve.1.refs_0_, s16[160,128]{1,0:T(8,128)(2,1)S(1)} %collective-permute-done.5.refs_1_, f32[2,16,128]{2,1,0:T(8,128)S(1)} %get-tuple-element.23.refs_2_, f32[2,2,16,16,128]{4,3,2,1,0:T(8,128)S(1)} %get-tuple-element.24.refs_3_, ...), custom_call_target="tpu_custom_call" | custom-call | flops 1000000000 | bytes 4000000 | tf_op jit(solution)/shard_map/transmit/pallas_call | solution.py:820
  28.4 0.0 collective-permute-done.4.refs_1_
  28.4 0.0 collective-permute-done.3.refs_0_
  28.4 3.8 %transmit.3 = f32[16,2,32,2,128]{4,3,2,1,0:T(2,128)} custom-call(s16[160,128]{1,0:T(8,128)(2,1)S(1)} %collective-permute-done.3.refs_0_, s16[160,128]{1,0:T(8,128)(2,1)S(1)} %collective-permute-done.4.refs_1_, f32[2,16,128]{2,1,0:T(8,128)S(1)} %get-tuple-element.23.refs_2_, f32[2,2,16,16,128]{4,3,2,1,0:T(8,128)S(1)} %get-tuple-element.24.refs_3_, ...), custom_call_target="tpu_custom_call" | custom-call | flops 1000000000 | bytes 4000000 | tf_op jit(solution)/shard_map/transmit/pallas_call | solution.py:820
Async XLA Ops:
  0.0 25.7 %copy-start = (f32[8,24,128]{2,1,0:T(8,128)S(1)}, f32[8,24,128]{2,1,0:T(8,128)}, u32[]{:S(2)}) copy-start(f32[8,24,128]{2,1,0:T(8,128)} %constant.5.clone.refs_7_) | copy-start | bytes 294916
  2.8 9.6 %collective-permute-start = (s16[144,128]{1,0:T(8,128)(2,1)S(1)}, s16[144,128]{1,0:T(8,128)(2,1)S(1)}, u32[]{:S(2)}, u32[]{:S(2)}) collective-permute-start(s16[144,128]{1,0:T(8,128)(2,1)S(1)} %get-tuple-element.19), channel_id=1, source_target_pairs={{0,3},{1,2},{2,1},{3,0},{4,7},{5,6},{6,5},{7,4},{8,11},{9,10},{10,... | collective-permute-start | bytes 110600 | tf_op jit(solution)/shard_map/ppermute | solution.py:733
  8.0 8.3 %all-to-all-start = ((f32[8,1,128]{2,1,0:T(1,128)}), f32[8,1,128]{2,1,0:T(1,128)S(1)}, u32[]{:S(2)}, u32[]{:S(2)}) async-start(f32[8,1,128]{2,1,0:T(1,128)} %get-tuple-element.16), calls=%async_computation | async-start | bytes 8192 | tf_op jit(solution)/shard_map/all_to_all | solution.py:773
  11.7 4.6 %collective-permute-start.1 = (s16[144,128]{1,0:T(8,128)(2,1)S(1)}, s16[144,128]{1,0:T(8,128)(2,1)S(1)}, u32[]{:S(2)}, u32[]{:S(2)}) collective-permute-start(s16[144,128]{1,0:T(8,128)(2,1)S(1)} %get-tuple-element.21), channel_id=1, source_target_pairs={{0,1},{1,0},{2,3},{3,2},{4,5},{5,4},{6,7},{7,6},{8,9},{9,8},{10,11... | collective-permute-start | bytes 110600 | tf_op jit(solution)/shard_map/ppermute | solution.py:733
  11.7 4.9 %collective-permute-start.2 = (s16[144,128]{1,0:T(8,128)(2,1)S(1)}, s16[144,128]{1,0:T(8,128)(2,1)S(1)}, u32[]{:S(2)}, u32[]{:S(2)}) collective-permute-start(s16[144,128]{1,0:T(8,128)(2,1)S(1)} %get-tuple-element.22), channel_id=1, source_target_pairs={{0,2},{1,3},{2,0},{3,1},{4,6},{5,7},{6,4},{7,5},{8,10},{9,11},{10,... | collective-permute-start | bytes 110600 | tf_op jit(solution)/shard_map/ppermute | solution.py:733
  19.9 5.8 %collective-permute-start.5 = (s16[160,128]{1,0:T(8,128)(2,1)S(1)}, s16[160,128]{1,0:T(8,128)(2,1)S(1)}, u32[]{:S(2)}, u32[]{:S(2)}) collective-permute-start(s16[160,128]{1,0:T(8,128)(2,1)S(1)} %solve.1.refs_0_), channel_id=1, source_target_pairs={{0,2},{1,3},{2,0},{3,1},{4,6},{5,7},{6,4},{7,5},{8,10},{9,11},{10,... | collective-permute-start | bytes 122888 | tf_op jit(solution)/shard_map/ppermute | solution.py:733
  21.0 7.4 %collective-permute-start.4 = (s16[160,128]{1,0:T(8,128)(2,1)S(1)}, s16[160,128]{1,0:T(8,128)(2,1)S(1)}, u32[]{:S(2)}, u32[]{:S(2)}) collective-permute-start(s16[160,128]{1,0:T(8,128)(2,1)S(1)} %solve.1.refs_0_), channel_id=1, source_target_pairs={{0,3},{1,2},{2,1},{3,0},{4,7},{5,6},{6,5},{7,4},{8,11},{9,10},{10,... | collective-permute-start | bytes 122888 | tf_op jit(solution)/shard_map/ppermute | solution.py:733
  24.3 4.1 %collective-permute-start.3 = (s16[160,128]{1,0:T(8,128)(2,1)S(1)}, s16[160,128]{1,0:T(8,128)(2,1)S(1)}, u32[]{:S(2)}, u32[]{:S(2)}) collective-permute-start(s16[160,128]{1,0:T(8,128)(2,1)S(1)} %solve.1.refs_0_), channel_id=1, source_target_pairs={{0,1},{1,0},{2,3},{3,2},{4,5},{5,4},{6,7},{7,6},{8,9},{9,8},{10,11... | collective-permute-start | bytes 122888 | tf_op jit(solution)/shard_map/ppermute | solution.py:733

commit v5 on v4

--- a/solution.py
+++ b/solution.py
@@ -36,14 +36,6 @@
 def turn(value, shift):
     shift = shift % WIDE
     return value if shift == 0 else pltpu.roll(value, shift, 1)
-
-
-def mirrored(index, lanes):
-    bits = lanes.bit_length() - 1
-    total = 0
-    for b in range(bits):
-        total = total + ((index >> b) % 2) * (1 << (bits - 1 - b))
-    return total
 
 
 def split(value, unit):
@@ -127,7 +119,7 @@
             total = total + amp * amp
         sums.append(jnp.sum(total, axis=0, keepdims=True) / order)
     lane = lax.axis_index("lane")
-    start = mirrored(lane, lanes) * chunk
+    start = lane * chunk
     mine = jnp.broadcast_to(sums[0], (ROWS, WIDE))
     for t in range(1, tiles):
         mine = jnp.where(start // WIDE == t, jnp.broadcast_to(sums[t], (ROWS, WIDE)), mine)
@@ -164,7 +156,7 @@
             return jnp.where(low, turn(top, -off), turn(bottom, HALF - off))
 
         for z in chunks:
-            pieces[lane ^ mirrored(z, lanes), pl.ds(order * ROWS, order), :] = split(
+            pieces[lane ^ z, pl.ds(order * ROWS, order), :] = split(
                 packed(root[0], root[1], z), ROOT_UNIT
             )
         for base in range(0, ROWS, 2):
@@ -211,7 +203,7 @@
                     value = jnp.concatenate(
                         [packed(tops_out[h], bottoms_out[h], z) for h in range(2)], 0
                     )
-                    pieces[lane ^ mirrored(z, lanes), pl.ds(l * order, order), :] = (
+                    pieces[lane ^ z, pl.ds(l * order, order), :] = (
                         jnp.round(value).astype(jnp.int32).astype(jnp.int16)
                     )
     for s in range(lanes):
@@ -492,7 +484,7 @@
         sum_ref[pl.ds((l * 2 + h) * ROWS, ROWS), :] = value + other[l, h]
 
 
-def transmit_kernel(*refs, which, last, lanes_count, chunk):
+def transmit_kernel(*refs, which, last, chunk):
     per_tile = WIDE // chunk
     ins, rest = refs[:per_tile], refs[per_tile:]
     amp, chan, sym, sums, table_ref, twist = rest[:6]
@@ -507,7 +499,7 @@
     per_block, syms = sym.shape[1], sym.shape[2] // (2 * order)
     groups = antennas // ROWS
     lanes = lane_iota()
-    lane = mirrored(lax.axis_index("lane"), lanes_count)
+    lane = lax.axis_index("lane")
     tile = (lane // per_tile) ^ which
     halves = [
         pltpu.make_async_copy(
@@ -807,7 +799,6 @@
         name="solve",
     )(near(transmit), near(mix), *map(near, parts))
     packs = swap([packed] * lanes)
-    packs = [packs[mirrored(i, lanes)] for i in range(lanes)]
 
     per_tile = WIDE // chunk
     height = syms * antennas
@@ -818,9 +809,7 @@
         result = (count, 4, 2, height, WIDE)
         final = (antennas, 2, NFFT // WIDE, syms, WIDE)
         out = pl.pallas_call(
-            functools.partial(
-                transmit_kernel, which=which, last=last, lanes_count=lanes, chunk=chunk
-            ),
+            functools.partial(transmit_kernel, which=which, last=last, chunk=chunk),
             out_shape=[shape(final, f32) if last else pltpu.VMEM(result, f32)],
             in_specs=[VMEM] * (per_tile + 4) + [HBM, VMEM] + [VMEM] * which,
             out_specs=[HBM if last else VMEM],

time: 32.4 us -> 31.8 us (0.981)
  starting transfers between devices: 14 us -> 13.2 us
    ppermute x6, starting transfers between devices: 10.3 us -> 9.45 us  [swap(): lax.ppermute(pieces[s], 'lane', [(j, j ^ s) for j in range(lanes)])]
  transfers between devices with their start and end apart: 7 -> 7, of which waited for: 3 -> 4; matrix products, arithmetic and copies ran while one was open for 0% -> 0% of each run, Pallas kernels for 16% -> 17%
where the time goes in v5:
time: 31.8 us; the launch traced here: 31.5 us
  Pallas kernels  15.1 us (47%)
  starting transfers between devices  13.2 us (42%)
  waiting for transfers between devices  3.27 us (10%)
    ppermute x6, starting transfers between devices, swap(): lax.ppermute(pieces[s], 'lane', [(j, j ^ s) for j in range(lanes)])  9.45 us
    pallas_call x2, Pallas kernels, per_device(): pl.pallas_call(functools.partial(transmit_kernel, which=which, last=last,...  6.41 us
    all_to_all x1, starting transfers between devices, per_device(): transmit = lax.all_to_all(own, 'cell', 0, 0, tiled=True)  3.72 us
    pallas_call x1, Pallas kernels, per_device(): pl.pallas_call(functools.partial(solve_kernel, count=lanes - 1), out_shap...  3.29 us
    pallas_call x1, Pallas kernels, per_device(): pl.pallas_call(functools.partial(gram_kernel, lanes=lanes, chunk=chunk),...  2.83 us
    pallas_call x1, Pallas kernels, per_device(): pl.pallas_call(arrange_kernel, out_shape=(pltpu.VMEM((tiles, sub, order *...  2.52 us
    ppermute x6, waiting for transfers between devices, swap(): lax.ppermute(pieces[s], 'lane', [(j, j ^ s) for j in range(lanes)])  2 us
    all_to_all x1, waiting for transfers between devices, per_device(): transmit = lax.all_to_all(own, 'cell', 0, 0, tiled=True)  1.27 us
  transfers between devices with their start and end apart: 7, of which 4 were waited for; matrix products, arithmetic and copies ran while one was open for 0% of the time, Pallas kernels for 17%

profile of v5, /device:TPU:0, one launch (start us, length us, event | category | flops | bytes accessed | tf_op | source)
XLA Modules:
  0.0 31.5 jit_solution(3621914033032287085)
XLA Ops:
  0.0 0.0 copy-start
  0.0 2.8 %gram.1 = (f32[2,16,128]{2,1,0:T(8,128)S(1)}, f32[8,1,128]{2,1,0:T(1,128)}, f32[8,1,128]{2,1,0:T(1,128)S(1)}, s16[144,128]{1,0:T(8,128)(2,1)S(1)}, s16[144,128]{...) custom-call(f32[1,16,2,16,256]{4,3,2,1,0:T(8,128)} %channel_ref.1, s32[1,256]{1,0:T(1,128)} %refs_1_.1, ...), custom_call_target="tpu_custom_call" | custom-call | tf_op jit(solution)/shard_map/gram/pallas_call | solution.py:743
  2.8 5.1 %collective-permute-start = (s16[144,128]{1,0:T(8,128)(2,1)S(1)}, s16[144,128]{1,0:T(8,128)(2,1)S(1)}, u32[]{:S(2)}, u32[]{:S(2)}) collective-permute-start(s16[144,128]{1,0:T(8,128)(2,1)S(1)} %get-tuple-element.19), channel_id=1, source_target_pairs={{0,3},{1,2},{2,1},{3,0},{4,7},{5,6},{6,5},{7,4},{8,11},{9,10},{10,... | collective-permute-start | bytes 110600 | tf_op jit(solution)/shard_map/ppermute | solution.py:725
  8.0 3.7 %all-to-all-start = ((f32[8,1,128]{2,1,0:T(1,128)}), f32[8,1,128]{2,1,0:T(1,128)S(1)}, u32[]{:S(2)}, u32[]{:S(2)}) async-start(f32[8,1,128]{2,1,0:T(1,128)} %get-tuple-element.16), calls=%async_computation | async-start | bytes 8192 | tf_op jit(solution)/shard_map/all_to_all | solution.py:765
  11.7 0.0 collective-permute-start.1
  11.7 0.8 %collective-permute-start.2 = (s16[144,128]{1,0:T(8,128)(2,1)S(1)}, s16[144,128]{1,0:T(8,128)(2,1)S(1)}, u32[]{:S(2)}, u32[]{:S(2)}) collective-permute-start(s16[144,128]{1,0:T(8,128)(2,1)S(1)} %get-tuple-element.22), channel_id=1, source_target_pairs={{0,2},{1,3},{2,0},{3,1},{4,6},{5,7},{6,4},{7,5},{8,10},{9,11},{10,... | collective-permute-start | bytes 110600 | tf_op jit(solution)/shard_map/ppermute | solution.py:725
  12.5 0.0 collective-permute-done.other_ref
  12.5 2.5 %arrange.1 = (f32[2,12,64,128]{3,2,1,0:T(8,128)S(1)}, f32[2,12,64,128]{3,2,1,0:T(8,128)S(1)}, f32[2,2,16,16,128]{4,3,2,1,0:T(8,128)S(1)}, f32[128,128]{1,0:T(8,128)S(1)}) custom-call(bf16[1,16,2,2,3072]{4,3,2,1,0:T(2,128)(2,1)} %far_ref.1, f32[1,16,2,16,256]{4,3,2,1,0:T(8,128)} %channel_ref.1, s16[144,128]{1,0:T(8,128)(2,1)S(1)} %get-tuple-element.18.own_ref, ...), custom_call_target="tpu_custom_call" | custom-call | flops 1000000000 | bytes 8000000 | tf_op jit(solution)/shard_map/arrange/pallas_call | solution.py:767
  15.0 1.3 %all-to-all-done.refs_0_ = f32[8,1,128]{2,1,0:T(1,128)S(1)} async-done(((f32[8,1,128]{2,1,0:T(1,128)}), f32[8,1,128]{2,1,0:T(1,128)S(1)}, u32[]{:S(2)}, u32[]{:S(2)}) %all-to-all-start) | async-done | bytes 4128 | tf_op jit(solution)/shard_map/all_to_all | solution.py:765
  16.3 0.0 collective-permute-done.1.refs_3_
  16.3 0.3 %collective-permute-done.2.refs_4_ = s16[144,128]{1,0:T(8,128)(2,1)S(1)} collective-permute-done((s16[144,128]{1,0:T(8,128)(2,1)S(1)}, s16[144,128]{1,0:T(8,128)(2,1)S(1)}, u32[]{:S(2)}, u32[]{:S(2)}) %collective-permute-start.2) | collective-permute-done | bytes 36896 | tf_op jit(solution)/shard_map/ppermute | solution.py:725
  16.6 3.3 %solve.1.refs_0_ = s16[160,128]{1,0:T(8,128)(2,1)S(1)} custom-call(f32[8,1,128]{2,1,0:T(1,128)S(1)} %all-to-all-done.refs_0_, f32[8,1,128]{2,1,0:T(1,128)S(1)} %get-tuple-element.17.refs_1_, f32[128,128]{1,0:T(8,128)S(1)} %get-tuple-element.20.refs_2_, s16[144,128]{1,0:T(8,128)(2,1)S(1)} %collective-permute-done.1.refs_3_, ...), custom_call_target="tpu_custom_call" | custom-call | tf_op jit(solution)/shard_map/solve/pallas_call | solution.py:792
  19.9 2.0 %collective-permute-start.5 = (s16[160,128]{1,0:T(8,128)(2,1)S(1)}, s16[160,128]{1,0:T(8,128)(2,1)S(1)}, u32[]{:S(2)}, u32[]{:S(2)}) collective-permute-start(s16[160,128]{1,0:T(8,128)(2,1)S(1)} %solve.1.refs_0_), channel_id=1, source_target_pairs={{0,1},{1,0},{2,3},{3,2},{4,5},{5,4},{6,7},{7,6},{8,9},{9,8},{10,11... | collective-permute-start | bytes 122888 | tf_op jit(solution)/shard_map/ppermute | solution.py:725
  21.9 0.5 %collective-permute-start.4 = (s16[160,128]{1,0:T(8,128)(2,1)S(1)}, s16[160,128]{1,0:T(8,128)(2,1)S(1)}, u32[]{:S(2)}, u32[]{:S(2)}) collective-permute-start(s16[160,128]{1,0:T(8,128)(2,1)S(1)} %solve.1.refs_0_), channel_id=1, source_target_pairs={{0,3},{1,2},{2,1},{3,0},{4,7},{5,6},{6,5},{7,4},{8,11},{9,10},{10,... | collective-permute-start | bytes 122888 | tf_op jit(solution)/shard_map/ppermute | solution.py:725
  22.5 1.0 %collective-permute-start.3 = (s16[160,128]{1,0:T(8,128)(2,1)S(1)}, s16[160,128]{1,0:T(8,128)(2,1)S(1)}, u32[]{:S(2)}, u32[]{:S(2)}) collective-permute-start(s16[160,128]{1,0:T(8,128)(2,1)S(1)} %solve.1.refs_0_), channel_id=1, source_target_pairs={{0,2},{1,3},{2,0},{3,1},{4,6},{5,7},{6,4},{7,5},{8,10},{9,11},{10,... | collective-permute-start | bytes 122888 | tf_op jit(solution)/shard_map/ppermute | solution.py:725
  23.5 0.5 %collective-permute-done.5.refs_1_ = s16[160,128]{1,0:T(8,128)(2,1)S(1)} collective-permute-done((s16[160,128]{1,0:T(8,128)(2,1)S(1)}, s16[160,128]{1,0:T(8,128)(2,1)S(1)}, u32[]{:S(2)}, u32[]{:S(2)}) %collective-permute-start.5) | collective-permute-done | bytes 40992 | tf_op jit(solution)/shard_map/ppermute | solution.py:725
  24.0 0.0 copy-done
  24.0 2.7 %transmit.2.refs_8_ = f32[8,4,2,32,128]{4,3,2,1,0:T(8,128)S(1)} custom-call(s16[160,128]{1,0:T(8,128)(2,1)S(1)} %solve.1.refs_0_, s16[160,128]{1,0:T(8,128)(2,1)S(1)} %collective-permute-done.5.refs_1_, f32[2,16,128]{2,1,0:T(8,128)S(1)} %get-tuple-element.23.refs_2_, f32[2,2,16,16,128]{4,3,2,1,0:T(8,128)S(1)} %get-tuple-element.24.refs_3_, ...), custom_call_target="tpu_custom_call" | custom-call | flops 1000000000 | bytes 4000000 | tf_op jit(solution)/shard_map/transmit/pallas_call | solution.py:811
  26.7 1.1 %collective-permute-done.4.refs_1_ = s16[160,128]{1,0:T(8,128)(2,1)S(1)} collective-permute-done((s16[160,128]{1,0:T(8,128)(2,1)S(1)}, s16[160,128]{1,0:T(8,128)(2,1)S(1)}, u32[]{:S(2)}, u32[]{:S(2)}) %collective-permute-start.4) | collective-permute-done | bytes 40992 | tf_op jit(solution)/shard_map/ppermute | solution.py:725
  27.8 0.0 collective-permute-done.3.refs_0_
  27.8 3.7 %transmit.3 = f32[16,2,32,2,128]{4,3,2,1,0:T(2,128)} custom-call(s16[160,128]{1,0:T(8,128)(2,1)S(1)} %collective-permute-done.3.refs_0_, s16[160,128]{1,0:T(8,128)(2,1)S(1)} %collective-permute-done.4.refs_1_, f32[2,16,128]{2,1,0:T(8,128)S(1)} %get-tuple-element.23.refs_2_, f32[2,2,16,16,128]{4,3,2,1,0:T(8,128)S(1)} %get-tuple-element.24.refs_3_, ...), custom_call_target="tpu_custom_call" | custom-call | flops 1000000000 | bytes 4000000 | tf_op jit(solution)/shard_map/transmit/pallas_call | solution.py:811
Async XLA Ops:
  0.0 24.0 %copy-start = (f32[8,24,128]{2,1,0:T(8,128)S(1)}, f32[8,24,128]{2,1,0:T(8,128)}, u32[]{:S(2)}) copy-start(f32[8,24,128]{2,1,0:T(8,128)} %constant.5.clone.refs_7_) | copy-start | bytes 294916
  2.8 9.6 %collective-permute-start = (s16[144,128]{1,0:T(8,128)(2,1)S(1)}, s16[144,128]{1,0:T(8,128)(2,1)S(1)}, u32[]{:S(2)}, u32[]{:S(2)}) collective-permute-start(s16[144,128]{1,0:T(8,128)(2,1)S(1)} %get-tuple-element.19), channel_id=1, source_target_pairs={{0,3},{1,2},{2,1},{3,0},{4,7},{5,6},{6,5},{7,4},{8,11},{9,10},{10,... | collective-permute-start | bytes 110600 | tf_op jit(solution)/shard_map/ppermute | solution.py:725
  8.0 8.3 %all-to-all-start = ((f32[8,1,128]{2,1,0:T(1,128)}), f32[8,1,128]{2,1,0:T(1,128)S(1)}, u32[]{:S(2)}, u32[]{:S(2)}) async-start(f32[8,1,128]{2,1,0:T(1,128)} %get-tuple-element.16), calls=%async_computation | async-start | bytes 8192 | tf_op jit(solution)/shard_map/all_to_all | solution.py:765
  11.7 4.6 %collective-permute-start.1 = (s16[144,128]{1,0:T(8,128)(2,1)S(1)}, s16[144,128]{1,0:T(8,128)(2,1)S(1)}, u32[]{:S(2)}, u32[]{:S(2)}) collective-permute-start(s16[144,128]{1,0:T(8,128)(2,1)S(1)} %get-tuple-element.21), channel_id=1, source_target_pairs={{0,1},{1,0},{2,3},{3,2},{4,5},{5,4},{6,7},{7,6},{8,9},{9,8},{10,11... | collective-permute-start | bytes 110600 | tf_op jit(solution)/shard_map/ppermute | solution.py:725
  11.7 4.9 %collective-permute-start.2 = (s16[144,128]{1,0:T(8,128)(2,1)S(1)}, s16[144,128]{1,0:T(8,128)(2,1)S(1)}, u32[]{:S(2)}, u32[]{:S(2)}) collective-permute-start(s16[144,128]{1,0:T(8,128)(2,1)S(1)} %get-tuple-element.22), channel_id=1, source_target_pairs={{0,2},{1,3},{2,0},{3,1},{4,6},{5,7},{6,4},{7,5},{8,10},{9,11},{10,... | collective-permute-start | bytes 110600 | tf_op jit(solution)/shard_map/ppermute | solution.py:725
  19.9 4.1 %collective-permute-start.5 = (s16[160,128]{1,0:T(8,128)(2,1)S(1)}, s16[160,128]{1,0:T(8,128)(2,1)S(1)}, u32[]{:S(2)}, u32[]{:S(2)}) collective-permute-start(s16[160,128]{1,0:T(8,128)(2,1)S(1)} %solve.1.refs_0_), channel_id=1, source_target_pairs={{0,1},{1,0},{2,3},{3,2},{4,5},{5,4},{6,7},{7,6},{8,9},{9,8},{10,11... | collective-permute-start | bytes 122888 | tf_op jit(solution)/shard_map/ppermute | solution.py:725
  21.9 5.9 %collective-permute-start.4 = (s16[160,128]{1,0:T(8,128)(2,1)S(1)}, s16[160,128]{1,0:T(8,128)(2,1)S(1)}, u32[]{:S(2)}, u32[]{:S(2)}) collective-permute-start(s16[160,128]{1,0:T(8,128)(2,1)S(1)} %solve.1.refs_0_), channel_id=1, source_target_pairs={{0,3},{1,2},{2,1},{3,0},{4,7},{5,6},{6,5},{7,4},{8,11},{9,10},{10,... | collective-permute-start | bytes 122888 | tf_op jit(solution)/shard_map/ppermute | solution.py:725
  22.5 5.3 %collective-permute-start.3 = (s16[160,128]{1,0:T(8,128)(2,1)S(1)}, s16[160,128]{1,0:T(8,128)(2,1)S(1)}, u32[]{:S(2)}, u32[]{:S(2)}) collective-permute-start(s16[160,128]{1,0:T(8,128)(2,1)S(1)} %solve.1.refs_0_), channel_id=1, source_target_pairs={{0,2},{1,3},{2,0},{3,1},{4,6},{5,7},{6,4},{7,5},{8,10},{9,11},{10,... | collective-permute-start | bytes 122888 | tf_op jit(solution)/shard_map/ppermute | solution.py:725
